TPU v7x, 32 devices: a whole 2x2x4 slice. The times are simulated.
32 devices in a mesh: dom: 2 (over x), space: 16 (over z, y, core).
Axes of the slice: x: 2, y: 2, z: 4, core: 2. Of those that a mesh axis runs over, the one named last changes fastest.
Arguments:
- inputs: bfloat16 [2, 32, 2048, 2048], P('dom', None, 'space'), parts along dimension 0, may hold values from -10.5 to 10.5
- target: bfloat16 [2, 32, 2048, 2048], P('dom', None, 'space'), parts along dimension 0, may hold values from -6 to 6
- spectral_weight: float32 [64, 32, 32, 128], P('space'), may hold values from -18 to 18
- local_weight: bfloat16 [32, 32], replicated, may hold values from -1 to 1
- bias_term: float32 [32], replicated, may hold values from -3 to 3
Outputs:
- grad_input: bfloat16 [2, 32, 2048, 2048], P('dom', None, 'space'), parts along dimension 0
- grad_spectral: float32 [64, 64, 32, 128], P('space', 'dom'), parts along dimension 1
- grad_local: float32 [64, 32], P('dom'), parts along dimension 0
- grad_bias: float32 [64], P('dom'), parts along dimension 0
There are 2 independent parts, one for each index of `dom`. A program takes and returns all parts, laid end to end along the dimension named above; an argument that names none is the same for every part. Nothing has to cross between parts.
All inputs are finite; a program needn't handle non-finite values.
Results may differ from a plain program's by a relative error of at most 0.014.
Values may be sent and summed in bfloat16 or wider, within the bound.
A program may use at most 192 MiB of HBM per device.

v0:
```python
import functools
import math

import jax
import jax.numpy as jnp
import ml_dtypes
import numpy as np
from jax import lax
from jax.experimental import pallas as pl
from jax.experimental.pallas import tpu as pltpu
from jax.sharding import PartitionSpec as P

KX = 64
KY = 64
LIMIT = 56 * 1024 * 1024
F32 = jnp.float32
BF16 = jnp.bfloat16


def row_table(height, width):
    angles = (np.arange(KY)[:, None] * np.arange(width)[None, :] % width) * (2.0 * math.pi / width)
    factor = 1.0 / math.sqrt(height * width)
    return np.concatenate([np.cos(angles) * factor, -np.sin(angles) * factor]).astype(ml_dtypes.bfloat16)


def column_table(height):
    column = np.arange(KX)
    frequency = np.where(column < KX // 2, column, column + height - KX)
    angles = (frequency[:, None] * np.arange(height)[None, :] % height) * (2.0 * math.pi / height)
    table = np.concatenate([np.cos(angles), -np.sin(angles)]).astype(np.float32)
    hi = table.astype(ml_dtypes.bfloat16)
    return hi, (table - hi.astype(np.float32)).astype(ml_dtypes.bfloat16)


def spread(weight, rows):
    flat = weight.shape[0] * rows
    place = jnp.arange(flat, dtype=jnp.int32)
    chosen = (place[:, None] // rows == jnp.arange(weight.shape[0])[None, :]).astype(BF16)
    wide = jnp.dot(jnp.dot(chosen, weight), chosen.T)
    return jnp.where(place[:, None] % rows == place[None, :] % rows, wide, 0.0).astype(BF16)


def column_parts(row_index, height):
    column = jnp.arange(KX, dtype=jnp.int32)
    frequency = jnp.where(column < KX // 2, column, column + height - KX)
    angles = (row_index[:, None] * frequency[None, :] % height).astype(F32) * (2.0 * math.pi / height)
    return jnp.cos(angles), jnp.sin(angles)


def split_hi_lo(value):
    hi = value.astype(BF16)
    return hi, (value - hi.astype(F32)).astype(BF16)


def dot3(a, b_hi, b_lo):
    a_hi, a_lo = split_hi_lo(a)
    mm = functools.partial(jnp.dot, preferred_element_type=F32)
    return mm(a_hi, b_hi) + (mm(a_lo, b_hi) + mm(a_hi, b_lo))


def columns_of(row_modes, b_hi, b_lo):
    turned = row_modes.T
    half = turned.shape[0] // 2
    both = jnp.concatenate([turned[:half], turned[half:]], axis=1)
    return dot3(both, b_hi, b_lo)


def analysis_kernel(x_ref, bt_ref, bh_ref, bl_ref, out_ref):
    count, rows, width = x_ref.shape
    flat = x_ref[...].reshape(count * rows, width)
    row_modes = jnp.dot(flat, bt_ref[...], preferred_element_type=F32)
    for c in range(count):
        out_ref[c] = columns_of(row_modes[c * rows : (c + 1) * rows], bh_ref[...], bl_ref[...])


def analysis(x, bt, b_hi, b_lo):
    chans, rows, width = x.shape
    block = 4
    whole = lambda a: pl.BlockSpec(a.shape, lambda i: (0,) * a.ndim)
    return pl.pallas_call(
        analysis_kernel,
        grid=(chans // block,),
        in_specs=[pl.BlockSpec((block, rows, width), lambda i: (i, 0, 0)), whole(bt), whole(b_hi), whole(b_lo)],
        out_specs=pl.BlockSpec((block, KY, 2 * KX), lambda i: (i, 0, 0)),
        out_shape=jax.ShapeDtypeStruct((chans, KY, 2 * KX), F32),
        compiler_params=pltpu.CompilerParams(vmem_limit_bytes=LIMIT),
        name="analysis",
    )(x, bt, b_hi, b_lo)


def halves(value):
    half = value.shape[-1] // 2
    return value[..., :half], value[..., half:]


def cat(a, b):
    return jnp.concatenate([a, b], axis=-1)


def synth_columns(z, cb_hi, cb_lo, e_ref):
    re, im = halves(z)
    devices, _, _, rows = e_ref.shape
    both = jnp.concatenate([z, cat(im, -re)], axis=0)
    z_hi, z_lo = split_hi_lo(both)
    count = z.shape[0]
    step = max(rows, min(512, devices * rows))
    mm = functools.partial(jnp.dot, preferred_element_type=F32)
    for start in range(0, devices * rows, step):
        cols = pl.ds(start, step)
        e = mm(z_hi, cb_hi[:, cols]) + (mm(z_lo, cb_hi[:, cols]) + mm(z_hi, cb_lo[:, cols]))
        e = e.astype(BF16)
        for d in range(step // rows):
            for p in range(2):
                e_ref[start // rows + d, p] = e[p * count : (p + 1) * count, d * rows : (d + 1) * rows]


def mix_kernel(r_ref, w_ref, gain_ref, ch_ref, cl_ref, e_ref, x_ref):
    modes = w_ref.shape[0]
    parts = []
    for k in range(modes):
        x = r_ref[0, k]
        for s in range(1, r_ref.shape[0]):
            x = x + r_ref[s, k]
        x_ref[k] = x
        re, im = halves(x)
        x_rr, x_ii = cat(re, re), cat(-im, im)
        total = jnp.zeros(w_ref.shape[2:], F32)
        for c in range(w_ref.shape[1]):
            w = w_ref[k, c]
            wr, wi = halves(w)
            total = total + x_rr[c : c + 1] * w + x_ii[c : c + 1] * cat(wi, wr)
        parts.append(total * gain_ref[k])
    synth_columns(jnp.concatenate(parts, axis=0), ch_ref, cl_ref, e_ref)


def back_kernel(r_ref, w_ref, gain_ref, ch_ref, cl_ref, x_ref, e_ref, g_ref, back_ref):
    modes, chans = w_ref.shape[:2]
    for k in range(modes):
        d = r_ref[0, k]
        for s in range(1, r_ref.shape[0]):
            d = d + r_ref[s, k]
        d = d * gain_ref[k]
        dr, di = halves(d)
        d_sw = cat(di, dr)
        re, im = halves(x_ref[k])
        x_rr, x_ii = cat(re, re), cat(im, -im)
        for c in range(chans):
            g_ref[k, c] = x_rr[c : c + 1] * d + x_ii[c : c + 1] * d_sw
            wr, wi = halves(w_ref[k, c])
            term = d * cat(wr, wr) + d_sw * cat(wi, -wi)
            back_ref[pl.ds(k * chans + c, 1), :] = jnp.sum(term, axis=0, keepdims=True)
    synth_columns(back_ref[...], ch_ref, cl_ref, e_ref)


def gelu_delta(v, target):
    e = jnp.exp2(v * v * (-0.5 / math.log(2.0)))
    d = 1.0 + jnp.abs(v) * (0.3275911 / math.sqrt(2.0))
    t = pl.reciprocal(d, approx=True)
    t = t * (2.0 - d * t)
    a = (0.254829592, -0.284496736, 1.421413741, -1.453152027, 1.061405429)
    q = 0.5 * a[4]
    for coef in (a[3], a[2], a[1], a[0]):
        q = q * t + 0.5 * coef
    tail = q * t * e
    phi = jnp.where(v >= 0.0, 1.0 - tail, tail)
    slope = phi + v * e * (1.0 / math.sqrt(2.0 * math.pi))
    return (v * phi - target) * slope


def forward_kernel(x_ref, t_ref, e_ref, kron_ref, bias_ref, rb_ref, bt_ref, bh_ref, bl_ref,
                   delta_ref, modes_ref, weight_ref, rows_ref, acc_ref):
    step = pl.program_id(0)
    chans, rows, width = x_ref.shape
    flat = chans * rows
    tile = 512
    nt = (((1,), (1,)), ((), ()))

    @pl.when(step == 0)
    def _():
        acc_ref[...] = jnp.zeros_like(acc_ref)

    e = e_ref[...].reshape(flat, e_ref.shape[2])
    row_modes = jnp.zeros((flat, bt_ref.shape[1]), F32)
    for start in range(0, width, tile):
        cols = pl.ds(start, tile)
        x = x_ref[:, :, cols].reshape(flat, tile)
        v = jnp.dot(e, rb_ref[:, cols], preferred_element_type=F32)
        v = v + jnp.dot(kron_ref[...], x, preferred_element_type=F32) + bias_ref[...]
        target = t_ref[:, :, cols].reshape(flat, tile).astype(F32)
        delta = gelu_delta(v, target).astype(BF16)
        delta_ref[:, :, cols] = delta.reshape(chans, rows, tile)
        row_modes = row_modes + jnp.dot(delta, bt_ref[cols, :], preferred_element_type=F32)
        acc_ref[...] += lax.dot_general(x, delta, nt, preferred_element_type=F32)
    rows_ref[:, pl.ds(pl.multiple_of(step * rows, rows), rows), :] = row_modes.reshape(chans, rows, -1)

    @pl.when(step == pl.num_programs(0) - 1)
    def _():
        def body(o, carry):
            modes_ref[o] = columns_of(rows_ref[o], bh_ref[...], bl_ref[...])
            return carry

        lax.fori_loop(0, chans, body, 0)
        first = lax.broadcasted_iota(jnp.int32, (flat, flat), 0)
        second = lax.broadcasted_iota(jnp.int32, (flat, flat), 1)
        kept = jnp.where(first % rows == second % rows, acc_ref[...], 0.0)
        weight_ref[...] = jnp.sum(kept.reshape(chans, rows, flat), axis=1)


def forward(x, target, e, kron, bias, rb, bt, b_hi, b_lo, rows):
    chans, slab, width = x.shape
    flat = chans * rows
    whole = lambda a: pl.BlockSpec(a.shape, lambda i: (0,) * a.ndim)
    band = lambda last: pl.BlockSpec((chans, rows, last), lambda i: (0, i, 0))
    return pl.pallas_call(
        forward_kernel,
        grid=(slab // rows,),
        in_specs=[band(width), band(width), band(e.shape[2]), whole(kron), whole(bias), whole(rb), whole(bt),
                  whole(b_hi), whole(b_lo)],
        out_specs=[
            band(width),
            pl.BlockSpec((chans, KY, 2 * KX), lambda i: (0, 0, 0)),
            pl.BlockSpec((chans, flat), lambda i: (0, 0)),
        ],
        out_shape=[
            jax.ShapeDtypeStruct(x.shape, BF16),
            jax.ShapeDtypeStruct((chans, KY, 2 * KX), F32),
            jax.ShapeDtypeStruct((chans, flat), F32),
        ],
        scratch_shapes=[pltpu.VMEM((chans, slab, 2 * KY), F32), pltpu.VMEM((flat, flat), F32)],
        compiler_params=pltpu.CompilerParams(vmem_limit_bytes=LIMIT),
        name="forward",
    )(x, target, e, kron, bias, rb, bt, b_hi, b_lo)


def final_kernel(d_ref, e_ref, kron_ref, rb_ref, out_ref):
    chans, rows, width = d_ref.shape
    flat = chans * rows
    tile = 512
    e = e_ref[...].reshape(flat, e_ref.shape[2])
    for start in range(0, width, tile):
        cols = pl.ds(start, tile)
        v = jnp.dot(e, rb_ref[:, cols], preferred_element_type=F32)
        d = d_ref[:, :, cols].reshape(flat, tile)
        v = v + jnp.dot(kron_ref[...], d, preferred_element_type=F32)
        out_ref[:, :, cols] = v.astype(BF16).reshape(chans, rows, tile)


def final(delta, e, kron, rb, rows):
    chans, slab, width = delta.shape
    whole = lambda a: pl.BlockSpec(a.shape, lambda i: (0,) * a.ndim)
    band = lambda last: pl.BlockSpec((chans, rows, last), lambda i: (0, i, 0))
    return pl.pallas_call(
        final_kernel,
        grid=(slab // rows,),
        in_specs=[band(width), band(e.shape[2]), whole(kron), whole(rb)],
        out_specs=band(width),
        out_shape=jax.ShapeDtypeStruct(delta.shape, BF16),
        compiler_params=pltpu.CompilerParams(vmem_limit_bytes=LIMIT),
        name="final",
    )(delta, e, kron, rb)


def per_device(inputs, target, spectral_weight, local_weight, bias_term):
    samples, chans, slab, width = inputs.shape
    devices = lax.axis_size("space")
    height = slab * devices
    own = spectral_weight.shape[0]
    device = lax.axis_index("space")
    rows = 16

    rb = row_table(height, width)
    bt = jnp.asarray(np.ascontiguousarray(rb.T))
    rb_in = jnp.asarray(rb.reshape(2, devices, own, width).transpose(1, 0, 2, 3).reshape(2 * KY, width))
    cosines, sines = column_parts(device * slab + jnp.arange(slab, dtype=jnp.int32), height)
    b_hi, b_lo = split_hi_lo(
        jnp.concatenate([cat(cosines, -sines), cat(sines, cosines)], axis=0)
    )
    c_hi, c_lo = (jnp.asarray(table) for table in column_table(height))
    mode = device * own + jnp.arange(own, dtype=jnp.int32)
    gain = jnp.broadcast_to(jnp.where(mode == 0, 1.0, 2.0).astype(F32)[:, None, None], (own, 1, 2 * KX))
    kron_out = spread(local_weight.T, rows)
    kron_back = spread(local_weight, rows)
    bias = jnp.repeat(bias_term, rows)[:, None]
    params = pltpu.CompilerParams(vmem_limit_bytes=LIMIT)
    e_shape = jax.ShapeDtypeStruct((devices, 2, own * chans, slab), BF16)
    x_shape = jax.ShapeDtypeStruct((own, chans, 2 * KX), F32)

    def by_owner(modes):
        return modes.reshape(chans, devices, own, 2 * KX).transpose(1, 2, 0, 3).reshape(devices, -1)

    def to_rows(e):
        got = lax.all_to_all(e, "space", split_axis=0, concat_axis=0, tiled=True)
        got = got.reshape(devices * 2 * own, chans, slab)
        return got.transpose(1, 2, 0)

    x = inputs.reshape(chans, slab, width)
    modes = by_owner(analysis(x, bt, b_hi, b_lo))
    got = lax.all_to_all(modes, "space", split_axis=0, concat_axis=0, tiled=True)
    e, own_modes = pl.pallas_call(
        mix_kernel, out_shape=[e_shape, x_shape], compiler_params=params, name="mix"
    )(got.reshape(devices, own, chans, 2 * KX), spectral_weight, gain, c_hi, c_lo)

    delta, delta_modes, weight_part = forward(
        x, target.reshape(chans, slab, width), to_rows(e), kron_out, bias, rb_in, bt, b_hi, b_lo, rows
    )
    weight_part = weight_part.reshape(chans, chans, rows).sum(axis=-1)
    bias_part = delta_modes[:, 0, 0] * math.sqrt(height * width)
    extra = jnp.concatenate([weight_part.reshape(-1), bias_part, jnp.zeros((992,), F32)])
    extra = jnp.broadcast_to(extra[None], (devices, extra.shape[0]))
    got = lax.all_to_all(by_owner(delta_modes), "space", split_axis=0, concat_axis=0, tiled=True)
    terms = lax.all_to_all(extra, "space", split_axis=0, concat_axis=0, tiled=True)
    e, grad_spectral = pl.pallas_call(
        back_kernel,
        out_shape=[e_shape, jax.ShapeDtypeStruct(spectral_weight.shape, F32)],
        scratch_shapes=[pltpu.VMEM((own * chans, 2 * KX), F32)],
        compiler_params=params,
        name="back",
    )(got.reshape(devices, own, chans, 2 * KX), spectral_weight, gain, c_hi, c_lo, own_modes)
    totals = jnp.sum(terms, axis=0) / (samples * height * width)
    grad_local = totals[: chans * chans].reshape(chans, chans)
    grad_bias = totals[chans * chans : chans * chans + chans]
    grad_input = final(delta, to_rows(e), kron_back, rb_in, rows)
    return (grad_input.reshape(inputs.shape), grad_spectral, grad_local, grad_bias)


def solution(mesh):
    return jax.shard_map(
        per_device,
        mesh=mesh,
        in_specs=(
            P("dom", None, "space", None),
            P("dom", None, "space", None),
            P("space", None, None, None),
            P(),
            P(),
        ),
        out_specs=(
            P("dom", None, "space", None),
            P("space", "dom", None, None),
            P("dom", None),
            P("dom"),
        ),
        check_vma=False,
    )
```

profile of v0, /device:TPU:0, one launch (start us, length us, event | category | flops | bytes accessed | tf_op | source)
XLA Modules:
  0.0 252.6 jit_solution(1472377615332245770)
XLA Ops:
  2.5 13.1 %analysis.1 = f32[32,64,128]{2,1,0:T(8,128)} custom-call(bf16[32,128,2048]{2,1,0:T(8,128)(2,1)} %bitcast.21, bf16[2048,128]{1,0:T(8,128)(2,1)} %constant.101.clone.bt_ref, bf16[256,128]{1,0:T(8,128)(2,1)} %fusion.11.bh_ref, bf16[256,128]{1,0:T(8,128)(2,1)} %subtract_convert_fusion.bl_ref), custom_call_target="tpu_custom_call" | custom-call | tf_op jit(solution)/shard_map/analysis/pallas_call | solution.py:80
  15.6 2.8 %copy.41 = f32[16,4,32,128]{3,2,1,0:T(8,128)} copy(f32[16,4,32,128]{3,1,0,2:T(4,128)} %bitcast.27) | data formatting | bytes 2097152 | tf_op jit(solution)/shard_map/transpose | solution.py:289
  18.4 7.4 %all-to-all-start = ((f32[16,1,16384]{2,1,0:T(1,128)}), f32[16,1,16384]{2,1,0:T(1,128)S(1)}, u32[]{:S(2)}, u32[]{:S(2)}) async-start(f32[16,1,16384]{2,1,0:T(1,128)} %bitcast.4), calls=%async_computation | async-start | bytes 2097152 | tf_op jit(solution)/shard_map/all_to_all | solution.py:298
  25.8 22.9 %all-to-all-done = f32[16,1,16384]{2,1,0:T(1,128)S(1)} async-done(((f32[16,1,16384]{2,1,0:T(1,128)}), f32[16,1,16384]{2,1,0:T(1,128)S(1)}, u32[]{:S(2)}, u32[]{:S(2)}) %all-to-all-start) | async-done | bytes 1048608 | tf_op jit(solution)/shard_map/all_to_all | solution.py:298
  49.7 4.7 %mix.1 = (bf16[16,2,128,128]{3,2,1,0:T(8,128)(2,1)}, f32[4,32,128]{2,1,0:T(8,128)}) custom-call(f32[16,4,32,128]{3,2,1,0:T(8,128)} %bitcast.31, f32[4,32,32,128]{3,2,1,0:T(8,128)} %w_ref.3, f32[4,1,128]{2,1,0:T(1,128)} %broadcast_in_dim.23.gain_ref, bf16[128,2048]{1,0:T(8,128)(2,1)} %constant.103.clone.ch_ref, bf16[128,2048]{1,0:T(8,128)(2,1)} %constant.104.clone.cl_ref), custom_call_target="tpu_custom_call" | custom-call | tf_op jit(solution)/shard_map/mix/pallas_call | solution.py:299
  54.5 6.9 %all-to-all-start.1 = ((bf16[16,2,128,128]{3,2,1,0:T(8,128)(2,1)}), bf16[16,2,128,128]{3,2,1,0:T(8,128)(2,1)S(1)}, u32[]{:S(2)}, u32[]{:S(2)}) async-start(bf16[16,2,128,128]{3,2,1,0:T(8,128)(2,1)} %get-tuple-element.11), calls=%async_computation.1 | async-start | bytes 2097152 | tf_op jit(solution)/shard_map/all_to_all | solution.py:292
  61.4 0.9 broadcast_in_dim_reshape.4.bias_ref
  62.3 1.4 compare_select_fusion.1.kron_ref
  63.6 20.6 %all-to-all-done.1 = bf16[16,2,128,128]{3,2,1,0:T(8,128)(2,1)S(1)} async-done(((bf16[16,2,128,128]{3,2,1,0:T(8,128)(2,1)}), bf16[16,2,128,128]{3,2,1,0:T(8,128)(2,1)S(1)}, u32[]{:S(2)}, u32[]{:S(2)}) %all-to-all-start.1) | async-done | bytes 1048608 | tf_op jit(solution)/shard_map/all_to_all | solution.py:292
  84.3 1.7 copy.42
  86.0 70.4 %forward.1 = (bf16[32,128,2048]{2,1,0:T(8,128)(2,1)}, f32[32,64,128]{2,1,0:T(8,128)}, f32[32,512]{1,0:T(8,128)}) custom-call(bf16[32,128,2048]{2,1,0:T(8,128)(2,1)} %bitcast.22, bf16[32,128,2048]{2,1,0:T(8,128)(2,1)} %bitcast.23, bf16[32,128,128]{2,1,0:T(8,128)(2,1)} %bitcast.25, bf16[512,512]{1,0:T(8,128)(2,1)} %compare_select_fusion.1.kron_ref, ...), custom_call_target="tpu_custom_call" | custom-call | tf_op jit(solution)/shard_map/forward/pallas_call | solution.py:214
  156.4 2.8 %copy.44 = f32[16,4,32,128]{3,2,1,0:T(8,128)} copy(f32[16,4,32,128]{3,1,0,2:T(4,128)} %bitcast.32) | data formatting | bytes 2097152 | tf_op jit(solution)/shard_map/transpose | solution.py:289
  159.2 6.9 %all-to-all-start.2 = ((f32[16,1,16384]{2,1,0:T(1,128)}), f32[16,1,16384]{2,1,0:T(1,128)S(1)}, u32[]{:S(2)}, u32[]{:S(2)}) async-start(f32[16,1,16384]{2,1,0:T(1,128)} %bitcast.10), calls=%async_computation.2 | async-start | bytes 2097152 | tf_op jit(solution)/shard_map/all_to_all | solution.py:310
  166.1 1.0 copy.46
  167.2 1.2 multiply_reduce_fusion
  168.6 20.5 %all-to-all-done.2 = f32[16,1,16384]{2,1,0:T(1,128)S(1)} async-done(((f32[16,1,16384]{2,1,0:T(1,128)}), f32[16,1,16384]{2,1,0:T(1,128)S(1)}, u32[]{:S(2)}, u32[]{:S(2)}) %all-to-all-start.2) | async-done | bytes 1048608 | tf_op jit(solution)/shard_map/all_to_all | solution.py:310
  189.8 6.9 %all-to-all-start.4 = ((f32[16,1,2048]{2,1,0:T(1,128)}), f32[16,1,2048]{2,1,0:T(1,128)S(1)}, u32[]{:S(2)}, u32[]{:S(2)}) async-start(f32[16,1,2048]{2,1,0:T(1,128)} %broadcast_in_dim.47), calls=%async_computation.4 | async-start | bytes 262144 | tf_op jit(solution)/shard_map/all_to_all | solution.py:311
  196.7 5.1 %back.1 = (bf16[16,2,128,128]{3,2,1,0:T(8,128)(2,1)}, f32[4,32,32,128]{3,2,1,0:T(8,128)}) custom-call(f32[16,4,32,128]{3,2,1,0:T(8,128)} %bitcast.30, f32[4,32,32,128]{3,2,1,0:T(8,128)} %w_ref.3, f32[4,1,128]{2,1,0:T(1,128)} %broadcast_in_dim.23.gain_ref, bf16[128,2048]{1,0:T(8,128)(2,1)} %constant.103.clone.ch_ref, ...), custom_call_target="tpu_custom_call" | custom-call | tf_op jit(solution)/shard_map/back/pallas_call | solution.py:312
  201.8 2.8 %all-to-all-done.4 = f32[16,1,2048]{2,1,0:T(1,128)S(1)} async-done(((f32[16,1,2048]{2,1,0:T(1,128)}), f32[16,1,2048]{2,1,0:T(1,128)S(1)}, u32[]{:S(2)}, u32[]{:S(2)}) %all-to-all-start.4) | async-done | bytes 131104 | tf_op jit(solution)/shard_map/all_to_all | solution.py:311
  204.6 3.7 %all-to-all-start.3 = ((bf16[16,2,128,128]{3,2,1,0:T(8,128)(2,1)}), bf16[16,2,128,128]{3,2,1,0:T(8,128)(2,1)S(1)}, u32[]{:S(2)}, u32[]{:S(2)}) async-start(bf16[16,2,128,128]{3,2,1,0:T(8,128)(2,1)} %get-tuple-element.15), calls=%async_computation.3 | async-start | bytes 2097152 | tf_op jit(solution)/shard_map/all_to_all | solution.py:292
  208.3 1.4 compare_select_fusion.kron_ref
  211.0 20.2 %all-to-all-done.3 = bf16[16,2,128,128]{3,2,1,0:T(8,128)(2,1)S(1)} async-done(((bf16[16,2,128,128]{3,2,1,0:T(8,128)(2,1)}), bf16[16,2,128,128]{3,2,1,0:T(8,128)(2,1)S(1)}, u32[]{:S(2)}, u32[]{:S(2)}) %all-to-all-start.3) | async-done | bytes 1048608 | tf_op jit(solution)/shard_map/all_to_all | solution.py:292
  231.2 1.7 copy.45
  232.9 19.7 %final.1 = bf16[32,128,2048]{2,1,0:T(8,128)(2,1)} custom-call(bf16[32,128,2048]{2,1,0:T(8,128)(2,1)} %get-tuple-element.12.d_ref, bf16[32,128,128]{2,1,0:T(8,128)(2,1)} %bitcast.26, bf16[512,512]{1,0:T(8,128)(2,1)} %compare_select_fusion.kron_ref, bf16[128,2048]{1,0:T(8,128)(2,1)} %constant.102.clone.rb_ref), custom_call_target="tpu_custom_call" | custom-call | tf_op jit(solution)/shard_map/final/pallas_call | solution.py:252
  (28 shorter events, 5.3 us)
Async XLA Ops:
  0.6 61.7 %copy-start = (bf16[32,32]{1,0:T(8,128)(2,1)S(1)}, bf16[32,32]{1,0:T(8,128)(2,1)}, u32[]{:S(2)}) copy-start(bf16[32,32]{1,0:T(8,128)(2,1)} %param.12) | copy-start | bytes 6148
  0.6 60.7 %copy-start.3 = (f32[32]{0:T(128)S(1)}, f32[32]{0:T(128)}, u32[]{:S(2)}) copy-start(f32[32]{0:T(128)} %param.13) | copy-start | bytes 388
  18.4 30.3 %all-to-all-start = ((f32[16,1,16384]{2,1,0:T(1,128)}), f32[16,1,16384]{2,1,0:T(1,128)S(1)}, u32[]{:S(2)}, u32[]{:S(2)}) async-start(f32[16,1,16384]{2,1,0:T(1,128)} %bitcast.4), calls=%async_computation | async-start | bytes 2097152 | tf_op jit(solution)/shard_map/all_to_all | solution.py:298
  48.7 1.0 copy-start.2
  54.5 29.8 %all-to-all-start.1 = ((bf16[16,2,128,128]{3,2,1,0:T(8,128)(2,1)}), bf16[16,2,128,128]{3,2,1,0:T(8,128)(2,1)S(1)}, u32[]{:S(2)}, u32[]{:S(2)}) async-start(bf16[16,2,128,128]{3,2,1,0:T(8,128)(2,1)} %get-tuple-element.11), calls=%async_computation.1 | async-start | bytes 2097152 | tf_op jit(solution)/shard_map/all_to_all | solution.py:292
  159.2 29.8 %all-to-all-start.2 = ((f32[16,1,16384]{2,1,0:T(1,128)}), f32[16,1,16384]{2,1,0:T(1,128)S(1)}, u32[]{:S(2)}, u32[]{:S(2)}) async-start(f32[16,1,16384]{2,1,0:T(1,128)} %bitcast.10), calls=%async_computation.2 | async-start | bytes 2097152 | tf_op jit(solution)/shard_map/all_to_all | solution.py:310
  189.0 7.7 %copy-start.1 = (f32[16,1,16384]{2,1,0:T(1,128)}, f32[16,1,16384]{2,1,0:T(1,128)S(1)}, u32[]{:S(2)}) copy-start(f32[16,1,16384]{2,1,0:T(1,128)S(1)} %all-to-all-done.2) | copy-start | bytes 3145732
  189.8 14.8 %all-to-all-start.4 = ((f32[16,1,2048]{2,1,0:T(1,128)}), f32[16,1,2048]{2,1,0:T(1,128)S(1)}, u32[]{:S(2)}, u32[]{:S(2)}) async-start(f32[16,1,2048]{2,1,0:T(1,128)} %broadcast_in_dim.47), calls=%async_computation.4 | async-start | bytes 262144 | tf_op jit(solution)/shard_map/all_to_all | solution.py:311
  204.6 26.6 %all-to-all-start.3 = ((bf16[16,2,128,128]{3,2,1,0:T(8,128)(2,1)}), bf16[16,2,128,128]{3,2,1,0:T(8,128)(2,1)S(1)}, u32[]{:S(2)}, u32[]{:S(2)}) async-start(bf16[16,2,128,128]{3,2,1,0:T(8,128)(2,1)} %get-tuple-element.15), calls=%async_computation.3 | async-start | bytes 2097152 | tf_op jit(solution)/shard_map/all_to_all | solution.py:292
where the time goes:
time: 255 us; the launch traced here: 253 us
  Pallas kernels  113 us (44%)
  waiting for transfers between devices  87 us (34%)
  starting transfers between devices  31.6 us (12%)
  local copies, waits for them, and re-layouts  14.1 us (6%)
  other arithmetic  3.19 us (1%)
  matrix products  2.75 us (1%)
    pallas_call x1, Pallas kernels, forward(): pl.pallas_call(forward_kernel, grid=(slab // rows,), in_specs=[band(width...  70.4 us
    all_to_all x2, waiting for transfers between devices, to_rows(): got = lax.all_to_all(e, 'space', split_axis=0, concat_axis=0, tiled=True)  40.8 us
    all_to_all x1, waiting for transfers between devices, per_device(): lax.all_to_all(modes, 'space', split_axis=0, concat_axis=0, tiled=True)  22.9 us
    all_to_all x1, waiting for transfers between devices, per_device(): lax.all_to_all(by_owner(delta_modes), 'space', split_axis=0, concat_axis=...  20.5 us
    pallas_call x1, Pallas kernels, final(): pl.pallas_call(final_kernel, grid=(slab // rows,), in_specs=[band(width),...  19.7 us
    pallas_call x1, Pallas kernels, analysis(): pl.pallas_call(analysis_kernel, grid=(chans // block,), in_specs=[pl.Bloc...  13.1 us
    all_to_all x2, starting transfers between devices, to_rows(): got = lax.all_to_all(e, 'space', split_axis=0, concat_axis=0, tiled=True)  10.5 us
    all_to_all x1, starting transfers between devices, per_device(): lax.all_to_all(modes, 'space', split_axis=0, concat_axis=0, tiled=True)  7.38 us
  transfers between devices with their start and end apart: 5, of which 5 were waited for; matrix products, arithmetic and copies ran while one was open for 3% of the time, Pallas kernels for 2%

commit v1 on v0

v1 whole, which is shorter than its diff:
```python
import functools
import math

import jax
import jax.numpy as jnp
import ml_dtypes
import numpy as np
from jax import lax
from jax.experimental import pallas as pl
from jax.experimental.pallas import tpu as pltpu
from jax.sharding import PartitionSpec as P

KX = 64
KY = 64
LANES = 2 * KX
QUARTER = KY // 4
LIMIT = 56 * 1024 * 1024
ROWS = 16
F32 = jnp.float32
BF16 = jnp.bfloat16
NT = (((1,), (1,)), ((), ()))
dot = functools.partial(jnp.dot, preferred_element_type=F32)
dot_nt = functools.partial(lax.dot_general, dimension_numbers=NT, preferred_element_type=F32)


def mode_order(devices):
    own = KY // devices
    return np.arange(KY).reshape(devices // 4, 2, 2, own).transpose(2, 1, 0, 3).reshape(-1)


def row_table(height, width, order):
    angles = (order[:, None] * np.arange(width)[None, :] % width) * (2.0 * math.pi / width)
    factor = 1.0 / math.sqrt(height * width)
    return np.concatenate([np.cos(angles) * factor, -np.sin(angles) * factor]).astype(ml_dtypes.bfloat16)


def column_table(height, devices):
    column = np.arange(KX)
    frequency = np.where(column < KX // 2, column, column + height - KX)
    angles = (np.arange(height)[:, None] * frequency[None, :] % height) * (2.0 * math.pi / height)
    cosines, sines = np.cos(angles), np.sin(angles)
    parts = np.stack([np.concatenate([cosines, -sines], 1), np.concatenate([sines, cosines], 1)])
    slab = height // devices
    table = parts.reshape(2, devices, slab, LANES).transpose(1, 0, 2, 3).reshape(devices, 2 * slab, LANES)
    table = table.astype(np.float32)
    hi = table.astype(ml_dtypes.bfloat16)
    lo = (table - hi.astype(np.float32)).astype(ml_dtypes.bfloat16)
    return np.concatenate([hi, lo], axis=2)


def halves(value):
    half = value.shape[-1] // 2
    return value[..., :half], value[..., half:]


def cat(a, b):
    return jnp.concatenate([a, b], axis=-1)


def columns_of(row_modes, table):
    parts = []
    for value in row_modes:
        turned = value.T
        parts.append(cat(turned[:KY], turned[KY:]))
    both = jnp.concatenate(parts, axis=0).astype(BF16)
    hi, lo = halves(dot(both, table))
    return hi + lo


def expand_rows(z_ref, table, slab, e_ref):
    chans = z_ref.shape[2]
    left = table[:slab]
    pair = 2

    def body(i, carry):
        parts = []
        for k in range(pair):
            z = z_ref[:, :, i * pair + k].reshape(KY, LANES)
            re, im = halves(z)
            both = jnp.concatenate([z, cat(im, -re)], axis=0)
            parts.append(cat(both, both))
        out = dot_nt(left, jnp.concatenate(parts, axis=0)).astype(BF16)
        for k in range(pair):
            e_ref[i * pair + k] = out[:, k * 2 * KY : (k + 1) * 2 * KY]
        return carry

    lax.fori_loop(0, chans // pair, body, 0)


def place():
    devices = lax.axis_size("space")
    me = lax.axis_index("space")
    return devices // 4, me, lax.rem(me, 2), lax.rem(me // 2, 2), me // 4


def peers():
    nz, me, core, mid, z = place()
    across = me + 1 - 2 * core
    beside = me + 2 - 4 * mid
    along = [lax.rem(z + i, nz) for i in range(nz)]
    return across, beside, along, [a * 4 + mid * 2 + core for a in along]


def greet():
    across, beside, _, line = peers()
    barrier = pltpu.get_barrier_semaphore()
    for target in [across, beside] + line[1:]:
        pl.semaphore_signal(barrier, inc=1, device_id={"space": target}, device_id_type=pl.DeviceIdType.MESH)


def greeted():
    pl.semaphore_wait(pltpu.get_barrier_semaphore(), len(peers()[3]) + 1)


class Links:
    def __init__(self, send_sem, recv_sem):
        self.send_sem, self.recv_sem, self.used, self.copies = send_sem, recv_sem, 0, []

    def start(self, src, dst, target):
        copy = pltpu.make_async_remote_copy(
            src_ref=src,
            dst_ref=dst,
            send_sem=self.send_sem.at[self.used],
            recv_sem=self.recv_sem.at[self.used],
            device_id={"space": target},
            device_id_type=pl.DeviceIdType.MESH,
        )
        copy.start()
        self.used += 1
        self.copies.append(copy)
        return copy

    def finish(self):
        for copy in self.copies:
            copy.wait_send()


def exchange_scratch(devices, chans, own, small):
    nz = devices // 4
    count = 5 + 2 * (nz - 1) + (nz + 1 if small else 0)
    shapes = [
        pltpu.VMEM((2, 2, chans, QUARTER, LANES), BF16),
        pltpu.VMEM((2, chans, QUARTER, LANES), BF16),
        pltpu.VMEM((chans, QUARTER, LANES), BF16),
        pltpu.VMEM((chans, QUARTER, LANES), BF16),
        pltpu.VMEM((chans, QUARTER, LANES), F32),
        pltpu.VMEM((nz, own, chans, LANES), F32),
        pltpu.VMEM((nz, own, chans, LANES), BF16),
        pltpu.VMEM((nz, own, chans, LANES), BF16),
        pltpu.VMEM((nz, own, chans, LANES), BF16),
        pltpu.VMEM((2, 2, chans, QUARTER, LANES), BF16),
        pltpu.VMEM((own, chans, chans, LANES), F32),
        pltpu.SemaphoreType.DMA((count,)),
        pltpu.SemaphoreType.DMA((count,)),
        pltpu.SemaphoreType.DMA,
        pltpu.SemaphoreType.DMA,
    ]
    if small:
        shapes += [pltpu.VMEM((4, chans, LANES), F32), pltpu.VMEM((nz, chans, LANES), F32)]
    return shapes


def exchange(scratch, mix, own_ref, z_ref, small_ref=None):
    m, r1, s2, r2, acc, s3f, s3, r3, zg, zt = scratch[:10]
    nz, me, core, mid, z = place()
    across, beside, along, line = peers()
    chans = m.shape[2]
    own = s3.shape[1]
    links = Links(scratch[11], scratch[12])

    first = links.start(m.at[1 - core], r1, across)
    if small_ref is not None:
        sm, rz = scratch[15:17]
        small_first = links.start(sm.at[0], sm.at[1], across)
    first.wait_recv()
    s2[...] = (m[core, 1 - mid].astype(F32) + r1[1 - mid].astype(F32)).astype(BF16)
    second = links.start(s2, r2, beside)
    if small_ref is not None:
        small_first.wait_recv()
        sm[2] = sm[0] + sm[1]
        small_second = links.start(sm.at[2], sm.at[3], beside)
    acc[...] = m[core, mid].astype(F32) + r1[mid].astype(F32)
    second.wait_recv()
    acc[...] += r2[...].astype(F32)
    for a in range(nz):
        for k in range(own):
            block = acc[:, a * own + k, :]
            s3f[a, k] = block
            s3[a, k] = block.astype(BF16)
    sums = [links.start(s3.at[along[i]], r3.at[i], line[i]) for i in range(1, nz)]
    if small_ref is not None:
        small_second.wait_recv()
        rz[z] = sm[2] + sm[3]
        smalls = [links.start(rz.at[z], rz.at[z], line[i]) for i in range(1, nz)]
    for i in range(1, nz):
        sums[i - 1].wait_recv()
    for k in range(own):
        total = s3f[z, k]
        for i in range(1, nz):
            total = total + r3[i, k].astype(F32)
        own_ref[k] = total

    mix(own_ref, zg, z)
    gathered = [links.start(zg.at[z], zg.at[z], line[i]) for i in range(1, nz)]
    if small_ref is not None:
        for copy in smalls:
            copy.wait_recv()
        total = rz[0]
        for i in range(1, nz):
            total = total + rz[i]
        small_ref[...] = total
    for copy in gathered:
        copy.wait_recv()
    for a in range(nz):
        for k in range(own):
            acc[:, a * own + k, :] = zg[a, k].astype(F32)
    zt[core, mid] = acc[...].astype(BF16)
    side = links.start(zt.at[core, mid], zt.at[core, mid], beside)
    near = links.start(zt.at[core, mid], zt.at[core, mid], across)
    side.wait_recv()
    far = links.start(zt.at[core, 1 - mid], zt.at[core, 1 - mid], across)
    near.wait_recv()
    far.wait_recv()
    links.finish()
    z_ref[...] = zt[...]


def mode_gain(me, own, k):
    return jnp.where(me * own + k == 0, 1.0, 2.0).astype(F32)


def swap(value):
    a, b = halves(value)
    return cat(b, a)


def mix_forward(w_ref, me, x_ref, z_ref, z):
    own, chans = w_ref.shape[:2]
    for k in range(own):
        x = x_ref[k]
        x_sw = swap(x)
        first = jnp.zeros(w_ref.shape[2:], F32)
        second = jnp.zeros(w_ref.shape[2:], F32)
        for c in range(chans):
            w = w_ref[k, c]
            first = first + x[c : c + 1] * w
            second = second + x_sw[c : c + 1] * w
        a, b = halves(first)
        c, d = halves(second)
        z_ref[z, k] = (cat(a - b, c + d) * mode_gain(me, own, k)).astype(BF16)


def mix_back(w_ref, me, d_ref, z_ref, z):
    own, chans = w_ref.shape[:2]
    for k in range(own):
        d = d_ref[k] * mode_gain(me, own, k)
        d_ref[k] = d
        d_sw = swap(d)
        firsts, seconds = [], []
        for c in range(chans):
            w = w_ref[k, c]
            firsts.append(jnp.sum(d * w, axis=0, keepdims=True))
            seconds.append(jnp.sum(d_sw * w, axis=0, keepdims=True))
        a, b = halves(jnp.concatenate(firsts, axis=0))
        e, f = halves(jnp.concatenate(seconds, axis=0))
        z_ref[z, k] = cat(a + b, e - f).astype(BF16)


def analysis_kernel(x_ref, bt_ref, cols_ref, w_ref, z_ref, own_ref, cols, *scratch):
    step = pl.program_id(0)
    count, rows, width = x_ref.shape
    m, wv, w_sem, c_sem = scratch[0], scratch[10], scratch[13], scratch[14]
    me = lax.axis_index("space")
    weights = pltpu.make_async_copy(w_ref, wv, w_sem)
    table = pltpu.make_async_copy(cols_ref.at[me], cols, c_sem)

    @pl.when(step == 0)
    def _():
        greet()
        table.start()
        weights.start()
        table.wait()

    flat = x_ref[...].reshape(count * rows, width)
    row_modes = dot(flat, bt_ref[...])
    modes = columns_of([row_modes[c * rows : (c + 1) * rows] for c in range(count)], cols[...]).astype(BF16)
    for c in range(count):
        m[:, :, step * count + c] = modes[c * KY : (c + 1) * KY].reshape(2, 2, QUARTER, LANES)

    @pl.when(step == pl.num_programs(0) - 1)
    def _():
        greeted()
        weights.wait()
        exchange(scratch, functools.partial(mix_forward, wv, me), own_ref, z_ref)


def whole(a):
    return pl.BlockSpec(a.shape, lambda i: (0,) * a.ndim)


def held(shape):
    return pl.BlockSpec(shape, lambda i: (0,) * len(shape))


HBM = pl.BlockSpec(memory_space=pl.ANY)


def analysis(x, bt, cols, weight, devices):
    chans, rows, width = x.shape
    own = weight.shape[0]
    block = 4
    shapes = [
        jax.ShapeDtypeStruct((2, 2, chans, QUARTER, LANES), BF16),
        jax.ShapeDtypeStruct((own, chans, LANES), F32),
    ]
    return pl.pallas_call(
        analysis_kernel,
        grid=(chans // block,),
        in_specs=[pl.BlockSpec((block, rows, width), lambda i: (i, 0, 0)), whole(bt), HBM, HBM],
        out_specs=[held(s.shape) for s in shapes],
        out_shape=shapes,
        scratch_shapes=[pltpu.VMEM(cols.shape[1:], BF16)] + exchange_scratch(devices, chans, own, False),
        compiler_params=pltpu.CompilerParams(vmem_limit_bytes=LIMIT, collective_id=0, has_side_effects=True),
        name="analysis",
    )(x, bt, cols, weight)


def spread(weight, flip, scale):
    chans = weight.shape[0]
    flat = chans * ROWS
    chosen = lax.broadcasted_iota(jnp.int32, (flat, chans), 0) // ROWS == lax.broadcasted_iota(jnp.int32, (flat, chans), 1)
    chosen = jnp.where(chosen, 1.0, 0.0).astype(BF16)
    tall = (dot_nt if flip else dot)(chosen, weight).astype(BF16)
    wide = dot_nt(tall, chosen)
    first = lax.broadcasted_iota(jnp.int32, (flat, flat), 0) % ROWS
    second = lax.broadcasted_iota(jnp.int32, (flat, flat), 1) % ROWS
    return jnp.where(first == second, wide * scale, 0.0).astype(BF16)


PHI = (1.5954356609777183, 0.29438608777535386, -0.010105857224310238)


def twice_delta(s, target):
    q = s * s
    p = jnp.minimum(q, 9.0)
    p = (PHI[2] * p + PHI[1]) * p + PHI[0]
    a = 1.0 + jnp.tanh(s * p)
    e = jnp.exp2(q * (-2.0 / math.log(2.0)) + math.log2(4.0 / math.sqrt(2.0 * math.pi)))
    return (s * a - target) * (a + s * e)


def forward_kernel(x_ref, t_ref, z_ref, lw_ref, bias_ref, rb_ref, bt_ref, cols_ref, w_ref,
                   delta_ref, back_ref, dm_ref, small_ref, cols, kron, rows_ref, acc_ref, e_ref, *scratch):
    step = pl.program_id(0)
    chans, rows, width = x_ref.shape
    slab = rows_ref.shape[1]
    flat = chans * rows
    tile = 512
    m, wv, w_sem, c_sem = scratch[0], scratch[10], scratch[13], scratch[14]
    sm = scratch[15]
    me = lax.axis_index("space")
    weights = pltpu.make_async_copy(w_ref, wv, w_sem)
    table = pltpu.make_async_copy(cols_ref.at[me], cols, c_sem)

    @pl.when(step == 0)
    def _():
        greet()
        table.start()
        weights.start()
        acc_ref[...] = jnp.zeros_like(acc_ref)
        kron[...] = spread(lw_ref[...], True, 0.5)
        table.wait()
        expand_rows(z_ref, cols[...], slab, e_ref)

    band = pl.ds(pl.multiple_of(step * rows, rows), rows)
    e = (e_ref[:, band, :].reshape(flat, LANES).astype(F32) * 0.5).astype(BF16)
    row_modes = jnp.zeros((flat, bt_ref.shape[1]), F32)
    bias = jnp.broadcast_to((bias_ref[...] * 0.5)[:, None, :], (chans, rows, LANES)).reshape(flat, LANES)[:, :1]
    for start in range(0, width, tile):
        cells = pl.ds(start, tile)
        x = x_ref[:, :, cells].reshape(flat, tile)
        s = dot(e, rb_ref[:, cells]) + dot(kron[...], x) + bias
        target = t_ref[:, :, cells].reshape(flat, tile).astype(F32)
        delta = twice_delta(s, target).astype(BF16)
        delta_ref[:, :, cells] = delta.reshape(chans, rows, tile)
        row_modes = row_modes + dot(delta, bt_ref[cells, :])
        acc_ref[...] += dot_nt(x, delta)
    rows_ref[:, band, :] = (row_modes * 0.5).reshape(chans, rows, -1)

    @pl.when(step == pl.num_programs(0) - 1)
    def _():
        count = 4

        def body(i, carry):
            modes = columns_of([rows_ref[i * count + k] for k in range(count)], cols[...]).astype(BF16)
            for k in range(count):
                m[:, :, i * count + k] = modes[k * KY : (k + 1) * KY].reshape(2, 2, QUARTER, LANES)
            return carry

        lax.fori_loop(0, chans // count, body, 0)
        first = lax.broadcasted_iota(jnp.int32, (flat, flat), 0) % rows
        second = lax.broadcasted_iota(jnp.int32, (flat, flat), 1) % rows
        kept = jnp.where(first == second, acc_ref[...], 0.0)
        kept = jnp.sum(kept.reshape(chans, rows, flat), axis=1)
        group = lax.broadcasted_iota(jnp.int32, (flat, LANES), 0) // rows
        lane = lax.broadcasted_iota(jnp.int32, (flat, LANES), 1)
        group = jnp.where(group == lane, 0.5, 0.0).astype(BF16)
        hi = kept.astype(BF16)
        rest = kept - hi.astype(F32)
        lo = rest.astype(BF16)
        last = (rest - lo.astype(F32)).astype(BF16)
        terms = dot(hi, group) + (dot(lo, group) + dot(last, group))
        sums = jnp.sum(rows_ref[...], axis=1)[:, :1]
        lane = lax.broadcasted_iota(jnp.int32, (chans, LANES), 1)
        sm[0] = jnp.where(lane == chans, sums, terms)
        greeted()
        weights.wait()
        exchange(scratch, functools.partial(mix_back, wv, me), dm_ref, back_ref, small_ref)


def forward(x, target, z, local_weight, bias, rb, bt, cols, weight, devices):
    chans, slab, width = x.shape
    own = weight.shape[0]
    flat = chans * ROWS
    band = pl.BlockSpec((chans, ROWS, width), lambda i: (0, i, 0))
    shapes = [
        jax.ShapeDtypeStruct(x.shape, BF16),
        jax.ShapeDtypeStruct((2, 2, chans, QUARTER, LANES), BF16),
        jax.ShapeDtypeStruct((own, chans, LANES), F32),
        jax.ShapeDtypeStruct((chans, LANES), F32),
    ]
    return pl.pallas_call(
        forward_kernel,
        grid=(slab // ROWS,),
        in_specs=[band, band, whole(z), whole(local_weight), whole(bias), whole(rb), whole(bt), HBM, HBM],
        out_specs=[band] + [held(s.shape) for s in shapes[1:]],
        out_shape=shapes,
        scratch_shapes=[
            pltpu.VMEM(cols.shape[1:], BF16),
            pltpu.VMEM((flat, flat), BF16),
            pltpu.VMEM((chans, slab, 2 * KY), F32),
            pltpu.VMEM((flat, flat), F32),
            pltpu.VMEM((chans, slab, 2 * KY), BF16),
        ] + exchange_scratch(devices, chans, own, True),
        compiler_params=pltpu.CompilerParams(vmem_limit_bytes=LIMIT, collective_id=1, has_side_effects=True),
        name="forward",
    )(x, target, z, local_weight, bias, rb, bt, cols, weight)


def final_kernel(root, cells_count, d_ref, z_ref, lw_ref, rb_ref, cols_ref, xm_ref, dm_ref, small_ref,
                 out_ref, g_ref, local_ref, bias_ref, cols, kron, e_ref, c_sem):
    step = pl.program_id(0)
    chans, rows, width = d_ref.shape
    slab = e_ref.shape[1]
    flat = chans * rows
    tile = 512
    pairs = g_ref.shape[0]
    me = lax.axis_index("space")
    table = pltpu.make_async_copy(cols_ref.at[me], cols, c_sem)

    @pl.when(step == 0)
    def _():
        table.start()
        kron[...] = spread(lw_ref[...], False, 0.5)
        small = small_ref[...]
        local_ref[...] = small[:, :chans] * (1.0 / cells_count)
        column = small[:, chans : chans + 1] * (root / cells_count)
        eye = lax.broadcasted_iota(jnp.int32, (chans, chans), 0) == lax.broadcasted_iota(jnp.int32, (chans, chans), 1)
        bias_ref[...] = jnp.sum(jnp.where(eye, column, 0.0), axis=0, keepdims=True)
        table.wait()
        expand_rows(z_ref, cols[...], slab, e_ref)

    e = e_ref[:, pl.ds(pl.multiple_of(step * rows, rows), rows), :].reshape(flat, LANES)
    for start in range(0, width, tile):
        cells = pl.ds(start, tile)
        d = d_ref[:, :, cells].reshape(flat, tile)
        v = dot(e, rb_ref[:, cells]) + dot(kron[...], d)
        out_ref[:, :, cells] = v.astype(BF16).reshape(chans, rows, tile)
    for i in range(pairs):
        index = step * pairs + i
        x = xm_ref[pl.ds(index, 1), :]
        re, im = halves(x)
        d = dm_ref[index // chans]
        g_ref[i] = cat(re, re) * d + cat(im, -im) * swap(d)


def final(delta, z, local_weight, rb, cols, own_modes, delta_modes, small, height):
    chans, slab, width = delta.shape
    own = own_modes.shape[0]
    flat = chans * ROWS
    steps = slab // ROWS
    pairs = own * chans // steps
    band = pl.BlockSpec((chans, ROWS, width), lambda i: (0, i, 0))
    own_modes = own_modes.reshape(own * chans, LANES)
    cells_count = height * width
    return pl.pallas_call(
        functools.partial(final_kernel, math.sqrt(cells_count), cells_count),
        grid=(steps,),
        in_specs=[band, whole(z), whole(local_weight), whole(rb), HBM, whole(own_modes), whole(delta_modes), whole(small)],
        out_specs=[
            band,
            pl.BlockSpec((pairs, chans, LANES), lambda i: (i, 0, 0)),
            held((chans, chans)),
            held((1, chans)),
        ],
        out_shape=[
            jax.ShapeDtypeStruct(delta.shape, BF16),
            jax.ShapeDtypeStruct((own * chans, chans, LANES), F32),
            jax.ShapeDtypeStruct((chans, chans), F32),
            jax.ShapeDtypeStruct((1, chans), F32),
        ],
        scratch_shapes=[
            pltpu.VMEM(cols.shape[1:], BF16),
            pltpu.VMEM((flat, flat), BF16),
            pltpu.VMEM((chans, slab, 2 * KY), BF16),
            pltpu.SemaphoreType.DMA,
        ],
        compiler_params=pltpu.CompilerParams(vmem_limit_bytes=LIMIT),
        name="final",
    )(delta, z, local_weight, rb, cols, own_modes, delta_modes, small)


def per_device(inputs, target, spectral_weight, local_weight, bias_term):
    samples, chans, slab, width = inputs.shape
    devices = lax.axis_size("space")
    height = slab * devices

    table = row_table(height, width, mode_order(devices))
    rb = jnp.asarray(table)
    bt = jnp.asarray(np.ascontiguousarray(table.T))
    cols = jnp.asarray(column_table(height, devices))
    bias = jnp.broadcast_to(bias_term[:, None], (chans, LANES))

    x = inputs.reshape(chans, slab, width)
    z, own_modes = analysis(x, bt, cols, spectral_weight, devices)
    delta, z, delta_modes, small = forward(
        x, target.reshape(chans, slab, width), z, local_weight, bias, rb, bt, cols, spectral_weight, devices
    )
    grad_input, grad_spectral, grad_local, grad_bias = final(
        delta, z, local_weight, rb, cols, own_modes, delta_modes, small, height
    )
    return (
        grad_input.reshape(inputs.shape),
        grad_spectral.reshape(spectral_weight.shape),
        grad_local,
        grad_bias.reshape(chans),
    )


def solution(mesh):
    return jax.shard_map(
        per_device,
        mesh=mesh,
        in_specs=(
            P("dom", None, "space", None),
            P("dom", None, "space", None),
            P("space", None, None, None),
            P(),
            P(),
        ),
        out_specs=(
            P("dom", None, "space", None),
            P("space", "dom", None, None),
            P("dom", None),
            P("dom"),
        ),
        check_vma=False,
    )
```

time: 255 us -> 143 us (0.56)
  waiting for transfers between devices: 87 us -> 0 us
  starting transfers between devices: 31.6 us -> 0 us
  Pallas kernels: 113 us -> 140 us
  local copies, waits for them, and re-layouts: 14.1 us -> 1.33 us
  other arithmetic: 3.19 us -> 0 us
  matrix products: 2.75 us -> 0 us
    all_to_all x5 -> x0, waiting for transfers between devices: 87 us -> none  [the longest x2 40.8 us: to_rows(): got = lax.all_to_all(e, 'space', split_axis=0, concat_axis=0, tiled=True)]
    all_to_all x5 -> x0, starting transfers between devices: 31.6 us -> none  [the longest x2 10.5 us: to_rows(): got = lax.all_to_all(e, 'space', split_axis=0, concat_axis=0, tiled=True)]
    pallas_call x1, Pallas kernels: 13.1 us -> 36.6 us  [analysis(): pl.pallas_call(analysis_kernel, grid=(chans // block,), in_specs=[pl.Bloc...]
    transpose x2 -> x0, local copies, waits for them, and re-layouts: 5.61 us -> none  [by_owner(): modes.reshape(chans, devices, own, 2 * KX).transpose(1, 2, 0, 3)]
    pallas_call x4 -> x2, Pallas kernels: 100 us -> 104 us  [the longest x1 78.4 us: forward(): pl.pallas_call(forward_kernel, grid=(slab // ROWS,), in_specs=[band, band...]
    reshape x3 -> x0, local copies, waits for them, and re-layouts: 3.43 us -> none  [the longest x2 3.36 us: to_rows(): got = got.reshape(devices * 2 * own, chans, slab)]
    dot_general x2 -> x0, matrix products: 2.75 us -> none  [spread(): wide = jnp.dot(jnp.dot(chosen, weight), chosen.T)]
  transfers between devices with their start and end apart: 5 -> 0, of which waited for: 5 -> 0; matrix products, arithmetic and copies ran while one was open for 3% -> 0% of each run, Pallas kernels for 2% -> 0%
where the time goes in v1:
time: 143 us; the launch traced here: 142 us
  Pallas kernels  140 us (98%)
    pallas_call x1, Pallas kernels, forward(): pl.pallas_call(forward_kernel, grid=(slab // ROWS,), in_specs=[band, band...  78.4 us
    pallas_call x1, Pallas kernels, analysis(): pl.pallas_call(analysis_kernel, grid=(chans // block,), in_specs=[pl.Bloc...  36.6 us
    pallas_call x1, Pallas kernels, final(): pl.pallas_call(functools.partial(final_kernel, math.sqrt(cells_count), ce...  25.2 us

profile of v1, /device:TPU:0, one launch (start us, length us, event | category | flops | bytes accessed | tf_op | source)
XLA Modules:
  0.0 142.2 jit_solution(3346133180105210603)
XLA Ops:
  0.6 1.3 broadcast_in_dim.2.bias_ref
  2.0 36.6 %analysis.1 = (bf16[2,2,32,16,128]{4,3,2,1,0:T(8,128)(2,1)}, f32[4,32,128]{2,1,0:T(8,128)}) custom-call(bf16[32,128,2048]{2,1,0:T(8,128)(2,1)} %bitcast.6, bf16[2048,128]{1,0:T(8,128)(2,1)} %constant.7.clone.bt_ref, bf16[16,256,256]{2,1,0:T(8,128)(2,1)} %constant.8.clone.cols_ref, f32[4,32,32,128]{3,2,1,0:T(8,128)} %w_ref.3), custom_call_target="tpu_custom_call" | custom-call | tf_op jit(solution)/shard_map/analysis/pallas_call | solution.py:316
  38.6 78.4 %forward.1 = (bf16[32,128,2048]{2,1,0:T(8,128)(2,1)}, bf16[2,2,32,16,128]{4,3,2,1,0:T(8,128)(2,1)}, f32[4,32,128]{2,1,0:T(8,128)}, f32[32,128]{1,0:T(8,128)}) custom-call(bf16[32,128,2048]{2,1,0:T(8,128)(2,1)} %bitcast.7, bf16[32,128,2048]{2,1,0:T(8,128)(2,1)} %bitcast.8, bf16[2,2,32,16,128]{4,3,2,1,0:T(8,128)(2,1)} %get-tuple-element.14.z_ref, ...), custom_call_target="tpu_custom_call" | custom-call | tf_op jit(solution)/shard_map/forward/pallas_call | solution.py:432
  117.0 25.2 %final.1 = (bf16[32,128,2048]{2,1,0:T(8,128)(2,1)}, f32[128,32,128]{2,1,0:T(8,128)}, f32[32,32]{1,0:T(8,128)}, f32[1,32]{1,0:T(1,128)}) custom-call(bf16[32,128,2048]{2,1,0:T(8,128)(2,1)} %get-tuple-element.15.d_ref, bf16[2,2,32,16,128]{4,3,2,1,0:T(8,128)(2,1)} %get-tuple-element.16.z_ref, bf16[32,32]{1,0:T(8,128)(2,1)} %lw_ref.3, ...), custom_call_target="tpu_custom_call" | custom-call | tf_op jit(solution)/shard_map/final/pallas_call | solution.py:496

commit v2 on v1

--- a/solution.py
+++ b/solution.py
@@ -16,6 +16,7 @@
 QUARTER = KY // 4
 LIMIT = 56 * 1024 * 1024
 ROWS = 16
+GROUP = 8
 F32 = jnp.float32
 BF16 = jnp.bfloat16
 NT = (((1,), (1,)), ((), ()))
@@ -70,7 +71,7 @@
 def expand_rows(z_ref, table, slab, e_ref):
     chans = z_ref.shape[2]
     left = table[:slab]
-    pair = 2
+    pair = 8
 
     def body(i, carry):
         parts = []
@@ -327,14 +328,31 @@
 
 def spread(weight, flip, scale):
     chans = weight.shape[0]
-    flat = chans * ROWS
-    chosen = lax.broadcasted_iota(jnp.int32, (flat, chans), 0) // ROWS == lax.broadcasted_iota(jnp.int32, (flat, chans), 1)
+    flat = chans * GROUP
+    chosen = lax.broadcasted_iota(jnp.int32, (flat, chans), 0) // GROUP == lax.broadcasted_iota(jnp.int32, (flat, chans), 1)
     chosen = jnp.where(chosen, 1.0, 0.0).astype(BF16)
     tall = (dot_nt if flip else dot)(chosen, weight).astype(BF16)
     wide = dot_nt(tall, chosen)
-    first = lax.broadcasted_iota(jnp.int32, (flat, flat), 0) % ROWS
-    second = lax.broadcasted_iota(jnp.int32, (flat, flat), 1) % ROWS
+    first = lax.broadcasted_iota(jnp.int32, (flat, flat), 0) % GROUP
+    second = lax.broadcasted_iota(jnp.int32, (flat, flat), 1) % GROUP
     return jnp.where(first == second, wide * scale, 0.0).astype(BF16)
+
+
+def groups_of(value):
+    chans, rows, last = value.shape
+    return [value[:, g : g + GROUP].reshape(chans * GROUP, last) for g in range(0, rows, GROUP)]
+
+
+def joined(groups, chans):
+    return jnp.concatenate([g.reshape(chans, GROUP, g.shape[-1]) for g in groups], axis=1)
+
+
+def bias_block(bias):
+    hi = bias.astype(BF16).astype(F32)
+    mid = (bias - hi).astype(BF16).astype(F32)
+    lo = bias - hi - mid
+    lane = lax.broadcasted_iota(jnp.int32, bias.shape, 1)
+    return jnp.where(lane == 0, hi, jnp.where(lane == 1, mid, jnp.where(lane == 2, lo, 0.0))).astype(BF16)
 
 
 PHI = (1.5954356609777183, 0.29438608777535386, -0.010105857224310238)
@@ -354,7 +372,7 @@
     step = pl.program_id(0)
     chans, rows, width = x_ref.shape
     slab = rows_ref.shape[1]
-    flat = chans * rows
+    half = chans * GROUP
     tile = 512
     m, wv, w_sem, c_sem = scratch[0], scratch[10], scratch[13], scratch[14]
     sm = scratch[15]
@@ -373,23 +391,29 @@
         expand_rows(z_ref, cols[...], slab, e_ref)
 
     band = pl.ds(pl.multiple_of(step * rows, rows), rows)
-    e = (e_ref[:, band, :].reshape(flat, LANES).astype(F32) * 0.5).astype(BF16)
-    row_modes = jnp.zeros((flat, bt_ref.shape[1]), F32)
-    bias = jnp.broadcast_to((bias_ref[...] * 0.5)[:, None, :], (chans, rows, LANES)).reshape(flat, LANES)[:, :1]
+    e = (e_ref[:, band, :].astype(F32) * 0.5).astype(BF16)
+    bias = jnp.broadcast_to((bias_ref[...] * 0.5)[:, None, :], (chans, GROUP, LANES)).reshape(half, LANES)
+    bias = bias_block(bias)
+    left = [jnp.concatenate([kron[...], group, bias], axis=1) for group in groups_of(e)]
+    row_modes = [jnp.zeros((half, bt_ref.shape[1]), F32) for _ in left]
     for start in range(0, width, tile):
         cells = pl.ds(start, tile)
-        x = x_ref[:, :, cells].reshape(flat, tile)
-        s = dot(e, rb_ref[:, cells]) + dot(kron[...], x) + bias
-        target = t_ref[:, :, cells].reshape(flat, tile).astype(F32)
-        delta = twice_delta(s, target).astype(BF16)
-        delta_ref[:, :, cells] = delta.reshape(chans, rows, tile)
-        row_modes = row_modes + dot(delta, bt_ref[cells, :])
-        acc_ref[...] += dot_nt(x, delta)
-    rows_ref[:, band, :] = (row_modes * 0.5).reshape(chans, rows, -1)
+        xs = groups_of(x_ref[:, :, cells])
+        targets = groups_of(t_ref[:, :, cells].astype(F32))
+        deltas = []
+        for lhs, x, target in zip(left, xs, targets):
+            s = dot(lhs, jnp.concatenate([x, rb_ref[:, cells]], axis=0))
+            deltas.append(twice_delta(s, target))
+        delta = joined(deltas, chans).astype(BF16)
+        delta_ref[:, :, cells] = delta
+        for g, group in enumerate(groups_of(delta)):
+            row_modes[g] = row_modes[g] + dot(group, bt_ref[cells, :])
+            acc_ref[...] += dot_nt(xs[g], group)
+    rows_ref[:, band, :] = joined(row_modes, chans) * 0.5
 
     @pl.when(step == pl.num_programs(0) - 1)
     def _():
-        count = 4
+        count = 8
 
         def body(i, carry):
             modes = columns_of([rows_ref[i * count + k] for k in range(count)], cols[...]).astype(BF16)
@@ -398,12 +422,12 @@
             return carry
 
         lax.fori_loop(0, chans // count, body, 0)
-        first = lax.broadcasted_iota(jnp.int32, (flat, flat), 0) % rows
-        second = lax.broadcasted_iota(jnp.int32, (flat, flat), 1) % rows
+        first = lax.broadcasted_iota(jnp.int32, (half, half), 0) % GROUP
+        second = lax.broadcasted_iota(jnp.int32, (half, half), 1) % GROUP
         kept = jnp.where(first == second, acc_ref[...], 0.0)
-        kept = jnp.sum(kept.reshape(chans, rows, flat), axis=1)
-        group = lax.broadcasted_iota(jnp.int32, (flat, LANES), 0) // rows
-        lane = lax.broadcasted_iota(jnp.int32, (flat, LANES), 1)
+        kept = jnp.sum(kept.reshape(chans, GROUP, half), axis=1)
+        group = lax.broadcasted_iota(jnp.int32, (half, LANES), 0) // GROUP
+        lane = lax.broadcasted_iota(jnp.int32, (half, LANES), 1)
         group = jnp.where(group == lane, 0.5, 0.0).astype(BF16)
         hi = kept.astype(BF16)
         rest = kept - hi.astype(F32)
@@ -421,7 +445,7 @@
 def forward(x, target, z, local_weight, bias, rb, bt, cols, weight, devices):
     chans, slab, width = x.shape
     own = weight.shape[0]
-    flat = chans * ROWS
+    half = chans * GROUP
     band = pl.BlockSpec((chans, ROWS, width), lambda i: (0, i, 0))
     shapes = [
         jax.ShapeDtypeStruct(x.shape, BF16),
@@ -437,9 +461,9 @@
         out_shape=shapes,
         scratch_shapes=[
             pltpu.VMEM(cols.shape[1:], BF16),
-            pltpu.VMEM((flat, flat), BF16),
+            pltpu.VMEM((half, half), BF16),
             pltpu.VMEM((chans, slab, 2 * KY), F32),
-            pltpu.VMEM((flat, flat), F32),
+            pltpu.VMEM((half, half), F32),
             pltpu.VMEM((chans, slab, 2 * KY), BF16),
         ] + exchange_scratch(devices, chans, own, True),
         compiler_params=pltpu.CompilerParams(vmem_limit_bytes=LIMIT, collective_id=1, has_side_effects=True),
@@ -452,7 +476,6 @@
     step = pl.program_id(0)
     chans, rows, width = d_ref.shape
     slab = e_ref.shape[1]
-    flat = chans * rows
     tile = 512
     pairs = g_ref.shape[0]
     me = lax.axis_index("space")
@@ -470,12 +493,14 @@
         table.wait()
         expand_rows(z_ref, cols[...], slab, e_ref)
 
-    e = e_ref[:, pl.ds(pl.multiple_of(step * rows, rows), rows), :].reshape(flat, LANES)
+    e = e_ref[:, pl.ds(pl.multiple_of(step * rows, rows), rows), :]
+    left = [cat(kron[...], group) for group in groups_of(e)]
     for start in range(0, width, tile):
         cells = pl.ds(start, tile)
-        d = d_ref[:, :, cells].reshape(flat, tile)
-        v = dot(e, rb_ref[:, cells]) + dot(kron[...], d)
-        out_ref[:, :, cells] = v.astype(BF16).reshape(chans, rows, tile)
+        out = []
+        for lhs, d in zip(left, groups_of(d_ref[:, :, cells])):
+            out.append(dot(lhs, jnp.concatenate([d, rb_ref[:, cells]], axis=0)))
+        out_ref[:, :, cells] = joined(out, chans).astype(BF16)
     for i in range(pairs):
         index = step * pairs + i
         x = xm_ref[pl.ds(index, 1), :]
@@ -487,7 +512,6 @@
 def final(delta, z, local_weight, rb, cols, own_modes, delta_modes, small, height):
     chans, slab, width = delta.shape
     own = own_modes.shape[0]
-    flat = chans * ROWS
     steps = slab // ROWS
     pairs = own * chans // steps
     band = pl.BlockSpec((chans, ROWS, width), lambda i: (0, i, 0))
@@ -511,7 +535,7 @@
         ],
         scratch_shapes=[
             pltpu.VMEM(cols.shape[1:], BF16),
-            pltpu.VMEM((flat, flat), BF16),
+            pltpu.VMEM((chans * GROUP, chans * GROUP), BF16),
             pltpu.VMEM((chans, slab, 2 * KY), BF16),
             pltpu.SemaphoreType.DMA,
         ],
@@ -528,13 +552,16 @@
     table = row_table(height, width, mode_order(devices))
     rb = jnp.asarray(table)
     bt = jnp.asarray(np.ascontiguousarray(table.T))
+    ones = np.zeros((LANES, width), ml_dtypes.bfloat16)
+    ones[:3] = 1.0
+    rb_bias = jnp.asarray(np.concatenate([table, ones]))
     cols = jnp.asarray(column_table(height, devices))
     bias = jnp.broadcast_to(bias_term[:, None], (chans, LANES))
 
     x = inputs.reshape(chans, slab, width)
     z, own_modes = analysis(x, bt, cols, spectral_weight, devices)
     delta, z, delta_modes, small = forward(
-        x, target.reshape(chans, slab, width), z, local_weight, bias, rb, bt, cols, spectral_weight, devices
+        x, target.reshape(chans, slab, width), z, local_weight, bias, rb_bias, bt, cols, spectral_weight, devices
     )
     grad_input, grad_spectral, grad_local, grad_bias = final(
         delta, z, local_weight, rb, cols, own_modes, delta_modes, small, height

time: 143 us -> 122 us (0.85)
  Pallas kernels: 140 us -> 120 us
    pallas_call x1, Pallas kernels: 78.4 us -> 62.5 us  [forward(): pl.pallas_call(forward_kernel, grid=(slab // ROWS,), in_specs=[band, band...]
    pallas_call x1, Pallas kernels: 25.2 us -> 20.8 us  [final(): pl.pallas_call(functools.partial(final_kernel, math.sqrt(cells_count), ce...]
where the time goes in v2:
time: 122 us
  Pallas kernels  120 us (98%)
  local copies, waits for them, and re-layouts  1.33 us (1%)
    pallas_call x1, Pallas kernels, forward(): pl.pallas_call(forward_kernel, grid=(slab // ROWS,), in_specs=[band, band...  62.5 us
    pallas_call x1, Pallas kernels, analysis(): pl.pallas_call(analysis_kernel, grid=(chans // block,), in_specs=[pl.Bloc...  36.6 us
    pallas_call x1, Pallas kernels, final(): pl.pallas_call(functools.partial(final_kernel, math.sqrt(cells_count), ce...  20.8 us

profile of v2, /device:TPU:0, one launch (start us, length us, event | category | flops | bytes accessed | tf_op | source)
XLA Modules:
  0.0 121.9 jit_solution(10509627139586481330)
XLA Ops:
  0.6 1.3 %broadcast_in_dim.2.bias_ref = f32[32,128]{1,0:T(8,128)} broadcast(f32[32]{0:T(128)} %param.13), dimensions={0} | broadcast | bytes 16512 | tf_op jit(solution)/shard_map/broadcast_in_dim | solution.py:559
  2.0 36.6 %analysis.1 = (bf16[2,2,32,16,128]{4,3,2,1,0:T(8,128)(2,1)}, f32[4,32,128]{2,1,0:T(8,128)}) custom-call(bf16[32,128,2048]{2,1,0:T(8,128)(2,1)} %bitcast.6, bf16[2048,128]{1,0:T(8,128)(2,1)} %constant.9.clone.bt_ref, bf16[16,256,256]{2,1,0:T(8,128)(2,1)} %constant.11.clone.cols_ref, f32[4,32,32,128]{3,2,1,0:T(8,128)} %w_ref.3), custom_call_target="tpu_custom_call" | custom-call | tf_op jit(solution)/shard_map/analysis/pallas_call | solution.py:317
  38.6 62.5 %forward.1 = (bf16[32,128,2048]{2,1,0:T(8,128)(2,1)}, bf16[2,2,32,16,128]{4,3,2,1,0:T(8,128)(2,1)}, f32[4,32,128]{2,1,0:T(8,128)}, f32[32,128]{1,0:T(8,128)}) custom-call(bf16[32,128,2048]{2,1,0:T(8,128)(2,1)} %bitcast.7, bf16[32,128,2048]{2,1,0:T(8,128)(2,1)} %bitcast.8, bf16[2,2,32,16,128]{4,3,2,1,0:T(8,128)(2,1)} %get-tuple-element.14.z_ref, ...), custom_call_target="tpu_custom_call" | custom-call | tf_op jit(solution)/shard_map/forward/pallas_call | solution.py:456
  101.1 20.8 %final.1 = (bf16[32,128,2048]{2,1,0:T(8,128)(2,1)}, f32[128,32,128]{2,1,0:T(8,128)}, f32[32,32]{1,0:T(8,128)}, f32[1,32]{1,0:T(1,128)}) custom-call(bf16[32,128,2048]{2,1,0:T(8,128)(2,1)} %get-tuple-element.15.d_ref, bf16[2,2,32,16,128]{4,3,2,1,0:T(8,128)(2,1)} %get-tuple-element.16.z_ref, bf16[32,32]{1,0:T(8,128)(2,1)} %lw_ref.3, ...), custom_call_target="tpu_custom_call" | custom-call | tf_op jit(solution)/shard_map/final/pallas_call | solution.py:520

commit v3 on v2

--- a/solution.py
+++ b/solution.py
@@ -16,6 +16,7 @@
 QUARTER = KY // 4
 LIMIT = 56 * 1024 * 1024
 ROWS = 16
+BAND = 16
 GROUP = 8
 F32 = jnp.float32
 BF16 = jnp.bfloat16
@@ -309,7 +310,7 @@
 def analysis(x, bt, cols, weight, devices):
     chans, rows, width = x.shape
     own = weight.shape[0]
-    block = 4
+    block = 8
     shapes = [
         jax.ShapeDtypeStruct((2, 2, chans, QUARTER, LANES), BF16),
         jax.ShapeDtypeStruct((own, chans, LANES), F32),
@@ -359,11 +360,12 @@
 
 
 def twice_delta(s, target):
+    one = lambda value: jnp.asarray(value, BF16)
     q = s * s
-    p = jnp.minimum(q, 9.0)
-    p = (PHI[2] * p + PHI[1]) * p + PHI[0]
-    a = 1.0 + jnp.tanh(s * p)
-    e = jnp.exp2(q * (-2.0 / math.log(2.0)) + math.log2(4.0 / math.sqrt(2.0 * math.pi)))
+    p = jnp.minimum(q, one(9.0))
+    p = (one(PHI[2]) * p + one(PHI[1])) * p + one(PHI[0])
+    a = one(1.0) + jnp.tanh(s * p)
+    e = jnp.exp2(q * one(-2.0 / math.log(2.0)) + one(math.log2(4.0 / math.sqrt(2.0 * math.pi))))
     return (s * a - target) * (a + s * e)
 
 
@@ -390,26 +392,33 @@
         table.wait()
         expand_rows(z_ref, cols[...], slab, e_ref)
 
-    band = pl.ds(pl.multiple_of(step * rows, rows), rows)
-    e = (e_ref[:, band, :].astype(F32) * 0.5).astype(BF16)
     bias = jnp.broadcast_to((bias_ref[...] * 0.5)[:, None, :], (chans, GROUP, LANES)).reshape(half, LANES)
     bias = bias_block(bias)
-    left = [jnp.concatenate([kron[...], group, bias], axis=1) for group in groups_of(e)]
-    row_modes = [jnp.zeros((half, bt_ref.shape[1]), F32) for _ in left]
-    for start in range(0, width, tile):
-        cells = pl.ds(start, tile)
-        xs = groups_of(x_ref[:, :, cells])
-        targets = groups_of(t_ref[:, :, cells].astype(F32))
+    def one_band(i, carry):
+        first = pl.multiple_of(i * BAND, BAND)
+        here = pl.ds(first, BAND)
+        band = pl.ds(pl.multiple_of(step * rows + first, BAND), BAND)
+        e = (e_ref[:, band, :].astype(F32) * 0.5).astype(BF16)
+        left = [cat(group, bias) for group in groups_of(e)]
         deltas = []
-        for lhs, x, target in zip(left, xs, targets):
-            s = dot(lhs, jnp.concatenate([x, rb_ref[:, cells]], axis=0))
-            deltas.append(twice_delta(s, target))
-        delta = joined(deltas, chans).astype(BF16)
-        delta_ref[:, :, cells] = delta
-        for g, group in enumerate(groups_of(delta)):
-            row_modes[g] = row_modes[g] + dot(group, bt_ref[cells, :])
-            acc_ref[...] += dot_nt(xs[g], group)
-    rows_ref[:, band, :] = joined(row_modes, chans) * 0.5
+        for start in range(0, width, tile):
+            cells = pl.ds(start, tile)
+            sums = []
+            for lhs, x in zip(left, groups_of(x_ref[:, here, cells])):
+                sums.append(dot(kron[...], x) + dot(lhs, rb_ref[:, cells]))
+            delta = twice_delta(joined(sums, chans).astype(BF16), t_ref[:, here, cells])
+            delta_ref[:, here, cells] = delta
+            deltas.append(groups_of(delta))
+        row_modes = []
+        for g, x in enumerate(groups_of(x_ref[:, here, :])):
+            delta = jnp.concatenate([d[g] for d in deltas], axis=1)
+            both = dot_nt(jnp.concatenate([x, bt_ref[...]], axis=0), delta)
+            acc_ref[...] += both[:half]
+            row_modes.append(both[half:].T)
+        rows_ref[:, band, :] = joined(row_modes, chans) * 0.5
+        return carry
+
+    lax.fori_loop(0, rows // BAND, one_band, 0)
 
     @pl.when(step == pl.num_programs(0) - 1)
     def _():
@@ -493,14 +502,20 @@
         table.wait()
         expand_rows(z_ref, cols[...], slab, e_ref)
 
-    e = e_ref[:, pl.ds(pl.multiple_of(step * rows, rows), rows), :]
-    left = [cat(kron[...], group) for group in groups_of(e)]
-    for start in range(0, width, tile):
-        cells = pl.ds(start, tile)
-        out = []
-        for lhs, d in zip(left, groups_of(d_ref[:, :, cells])):
-            out.append(dot(lhs, jnp.concatenate([d, rb_ref[:, cells]], axis=0)))
-        out_ref[:, :, cells] = joined(out, chans).astype(BF16)
+    def one_band(i, carry):
+        first = pl.multiple_of(i * BAND, BAND)
+        here = pl.ds(first, BAND)
+        e = e_ref[:, pl.ds(pl.multiple_of(step * rows + first, BAND), BAND), :]
+        left = [cat(kron[...], group) for group in groups_of(e)]
+        for start in range(0, width, tile):
+            cells = pl.ds(start, tile)
+            out = []
+            for lhs, d in zip(left, groups_of(d_ref[:, here, cells])):
+                out.append(dot(lhs, jnp.concatenate([d, rb_ref[:, cells]], axis=0)))
+            out_ref[:, here, cells] = joined(out, chans).astype(BF16)
+        return carry
+
+    lax.fori_loop(0, rows // BAND, one_band, 0)
     for i in range(pairs):
         index = step * pairs + i
         x = xm_ref[pl.ds(index, 1), :]
@@ -561,7 +576,7 @@
     x = inputs.reshape(chans, slab, width)
     z, own_modes = analysis(x, bt, cols, spectral_weight, devices)
     delta, z, delta_modes, small = forward(
-        x, target.reshape(chans, slab, width), z, local_weight, bias, rb_bias, bt, cols, spectral_weight, devices
+        x, target.reshape(chans, slab, width), z, local_weight, bias, rb_bias, rb, cols, spectral_weight, devices
     )
     grad_input, grad_spectral, grad_local, grad_bias = final(
         delta, z, local_weight, rb, cols, own_modes, delta_modes, small, height

time: 122 us -> 114 us (0.934)
  Pallas kernels: 120 us -> 111 us
    pallas_call x1, Pallas kernels: 62.5 us -> 56.1 us  [forward(): pl.pallas_call(forward_kernel, grid=(slab // ROWS,), in_specs=[band, band...]
    pallas_call x1, Pallas kernels: 36.6 us -> 34.6 us  [analysis(): pl.pallas_call(analysis_kernel, grid=(chans // block,), in_specs=[pl.Bloc...]
where the time goes in v3:
time: 114 us; the launch traced here: 113 us
  Pallas kernels  111 us (97%)
  local copies, waits for them, and re-layouts  1.33 us (1%)
    pallas_call x1, Pallas kernels, forward(): pl.pallas_call(forward_kernel, grid=(slab // ROWS,), in_specs=[band, band...  56.1 us
    pallas_call x1, Pallas kernels, analysis(): pl.pallas_call(analysis_kernel, grid=(chans // block,), in_specs=[pl.Bloc...  34.6 us
    pallas_call x1, Pallas kernels, final(): pl.pallas_call(functools.partial(final_kernel, math.sqrt(cells_count), ce...  20.8 us

profile of v3, /device:TPU:0, one launch (start us, length us, event | category | flops | bytes accessed | tf_op | source)
XLA Modules:
  0.0 113.4 jit_solution(16510467170082058853)
XLA Ops:
  0.6 1.3 %broadcast_in_dim.2.bias_ref = f32[32,128]{1,0:T(8,128)} broadcast(f32[32]{0:T(128)} %param.13), dimensions={0} | broadcast | bytes 16512 | tf_op jit(solution)/shard_map/broadcast_in_dim | solution.py:574
  2.0 34.6 %analysis.1 = (bf16[2,2,32,16,128]{4,3,2,1,0:T(8,128)(2,1)}, f32[4,32,128]{2,1,0:T(8,128)}) custom-call(bf16[32,128,2048]{2,1,0:T(8,128)(2,1)} %bitcast.6, bf16[2048,128]{1,0:T(8,128)(2,1)} %constant.9.clone.bt_ref, bf16[16,256,256]{2,1,0:T(8,128)(2,1)} %constant.11.clone.cols_ref, f32[4,32,32,128]{3,2,1,0:T(8,128)} %w_ref.3), custom_call_target="tpu_custom_call" | custom-call | tf_op jit(solution)/shard_map/analysis/pallas_call | solution.py:318
  36.5 56.1 %forward.1 = (bf16[32,128,2048]{2,1,0:T(8,128)(2,1)}, bf16[2,2,32,16,128]{4,3,2,1,0:T(8,128)(2,1)}, f32[4,32,128]{2,1,0:T(8,128)}, f32[32,128]{1,0:T(8,128)}) custom-call(bf16[32,128,2048]{2,1,0:T(8,128)(2,1)} %bitcast.7, bf16[32,128,2048]{2,1,0:T(8,128)(2,1)} %bitcast.8, bf16[2,2,32,16,128]{4,3,2,1,0:T(8,128)(2,1)} %get-tuple-element.14.z_ref, ...), custom_call_target="tpu_custom_call" | custom-call | tf_op jit(solution)/shard_map/forward/pallas_call | solution.py:465
  92.6 20.8 %final.1 = (bf16[32,128,2048]{2,1,0:T(8,128)(2,1)}, f32[128,32,128]{2,1,0:T(8,128)}, f32[32,32]{1,0:T(8,128)}, f32[1,32]{1,0:T(1,128)}) custom-call(bf16[32,128,2048]{2,1,0:T(8,128)(2,1)} %get-tuple-element.15.d_ref, bf16[2,2,32,16,128]{4,3,2,1,0:T(8,128)(2,1)} %get-tuple-element.16.z_ref, bf16[32,32]{1,0:T(8,128)(2,1)} %lw_ref.3, ...), custom_call_target="tpu_custom_call" | custom-call | tf_op jit(solution)/shard_map/final/pallas_call | solution.py:535

commit v4 on v3

--- a/solution.py
+++ b/solution.py
@@ -18,6 +18,8 @@
 ROWS = 16
 BAND = 16
 GROUP = 8
+CHUNK = 8
+HALF = 16
 F32 = jnp.float32
 BF16 = jnp.bfloat16
 NT = (((1,), (1,)), ((), ()))
@@ -114,117 +116,199 @@
     pl.semaphore_wait(pltpu.get_barrier_semaphore(), len(peers()[3]) + 1)
 
 
-class Links:
-    def __init__(self, send_sem, recv_sem):
-        self.send_sem, self.recv_sem, self.used, self.copies = send_sem, recv_sem, 0, []
-
-    def start(self, src, dst, target):
-        copy = pltpu.make_async_remote_copy(
-            src_ref=src,
-            dst_ref=dst,
-            send_sem=self.send_sem.at[self.used],
-            recv_sem=self.recv_sem.at[self.used],
-            device_id={"space": target},
-            device_id_type=pl.DeviceIdType.MESH,
-        )
-        copy.start()
-        self.used += 1
-        self.copies.append(copy)
-        return copy
-
-    def finish(self):
-        for copy in self.copies:
-            copy.wait_send()
+def remote(src, dst, send_sem, recv_sem, target):
+    return pltpu.make_async_remote_copy(
+        src_ref=src,
+        dst_ref=dst,
+        send_sem=send_sem,
+        recv_sem=recv_sem,
+        device_id={"space": target},
+        device_id_type=pl.DeviceIdType.MESH,
+    )
 
 
 def exchange_scratch(devices, chans, own, small):
     nz = devices // 4
-    count = 5 + 2 * (nz - 1) + (nz + 1 if small else 0)
+    parts, wide = chans // CHUNK, chans // HALF
     shapes = [
-        pltpu.VMEM((2, 2, chans, QUARTER, LANES), BF16),
-        pltpu.VMEM((2, chans, QUARTER, LANES), BF16),
-        pltpu.VMEM((chans, QUARTER, LANES), BF16),
-        pltpu.VMEM((chans, QUARTER, LANES), BF16),
-        pltpu.VMEM((chans, QUARTER, LANES), F32),
-        pltpu.VMEM((nz, own, chans, LANES), F32),
-        pltpu.VMEM((nz, own, chans, LANES), BF16),
-        pltpu.VMEM((nz, own, chans, LANES), BF16),
-        pltpu.VMEM((nz, own, chans, LANES), BF16),
-        pltpu.VMEM((2, 2, chans, QUARTER, LANES), BF16),
+        pltpu.VMEM((parts, 2, 2, CHUNK, QUARTER, LANES), BF16),
+        pltpu.VMEM((parts, 2, CHUNK, QUARTER, LANES), BF16),
+        pltpu.VMEM((parts, CHUNK, QUARTER, LANES), BF16),
+        pltpu.VMEM((parts, CHUNK, QUARTER, LANES), BF16),
+        pltpu.VMEM((parts, CHUNK, QUARTER, LANES), F32),
+        pltpu.VMEM((parts, nz, own, CHUNK, LANES), F32),
+        pltpu.VMEM((parts, nz, own, CHUNK, LANES), BF16),
+        pltpu.VMEM((parts, nz, own, CHUNK, LANES), BF16),
+        pltpu.VMEM((wide, nz, own, HALF, LANES), BF16),
+        pltpu.VMEM((wide, HALF, QUARTER, LANES), F32),
+        pltpu.VMEM((wide, 2, 2, HALF, QUARTER, LANES), BF16),
         pltpu.VMEM((own, chans, chans, LANES), F32),
-        pltpu.SemaphoreType.DMA((count,)),
-        pltpu.SemaphoreType.DMA((count,)),
+        pltpu.SemaphoreType.DMA((nz + 1, parts)),
+        pltpu.SemaphoreType.DMA((nz + 1, parts)),
+        pltpu.SemaphoreType.DMA((nz + 2, wide)),
+        pltpu.SemaphoreType.DMA((nz + 2, wide)),
         pltpu.SemaphoreType.DMA,
         pltpu.SemaphoreType.DMA,
     ]
     if small:
-        shapes += [pltpu.VMEM((4, chans, LANES), F32), pltpu.VMEM((nz, chans, LANES), F32)]
+        shapes += [
+            pltpu.VMEM((4, chans, LANES), F32),
+            pltpu.VMEM((nz, chans, LANES), F32),
+            pltpu.SemaphoreType.DMA((nz + 1,)),
+            pltpu.SemaphoreType.DMA((nz + 1,)),
+        ]
     return shapes
 
 
-def exchange(scratch, mix, own_ref, z_ref, small_ref=None):
-    m, r1, s2, r2, acc, s3f, s3, r3, zg, zt = scratch[:10]
-    nz, me, core, mid, z = place()
-    across, beside, along, line = peers()
-    chans = m.shape[2]
-    own = s3.shape[1]
-    links = Links(scratch[11], scratch[12])
-
-    first = links.start(m.at[1 - core], r1, across)
-    if small_ref is not None:
-        sm, rz = scratch[15:17]
-        small_first = links.start(sm.at[0], sm.at[1], across)
-    first.wait_recv()
-    s2[...] = (m[core, 1 - mid].astype(F32) + r1[1 - mid].astype(F32)).astype(BF16)
-    second = links.start(s2, r2, beside)
-    if small_ref is not None:
-        small_first.wait_recv()
-        sm[2] = sm[0] + sm[1]
-        small_second = links.start(sm.at[2], sm.at[3], beside)
-    acc[...] = m[core, mid].astype(F32) + r1[mid].astype(F32)
-    second.wait_recv()
-    acc[...] += r2[...].astype(F32)
-    for a in range(nz):
-        for k in range(own):
-            block = acc[:, a * own + k, :]
-            s3f[a, k] = block
-            s3[a, k] = block.astype(BF16)
-    sums = [links.start(s3.at[along[i]], r3.at[i], line[i]) for i in range(1, nz)]
-    if small_ref is not None:
-        small_second.wait_recv()
-        rz[z] = sm[2] + sm[3]
-        smalls = [links.start(rz.at[z], rz.at[z], line[i]) for i in range(1, nz)]
-    for i in range(1, nz):
-        sums[i - 1].wait_recv()
-    for k in range(own):
-        total = s3f[z, k]
-        for i in range(1, nz):
-            total = total + r3[i, k].astype(F32)
-        own_ref[k] = total
-
-    mix(own_ref, zg, z)
-    gathered = [links.start(zg.at[z], zg.at[z], line[i]) for i in range(1, nz)]
-    if small_ref is not None:
-        for copy in smalls:
+class Sums:
+    def __init__(self, scratch):
+        self.m, self.r1, self.s2, self.r2, self.acc, self.s3f, self.s3, self.r3 = scratch[:8]
+        self.send_sem, self.recv_sem = scratch[12:14]
+        self.nz, _, self.core, self.mid, self.z = place()
+        self.across, self.beside, self.along, self.line = peers()
+
+    def copy(self, stage, c):
+        if stage == 0:
+            ends = self.m.at[c, 1 - self.core], self.r1.at[c], self.across
+        elif stage == 1:
+            ends = self.s2.at[c], self.r2.at[c], self.beside
+        else:
+            i = stage - 1
+            ends = self.s3.at[c, self.along[i]], self.r3.at[c, i], self.line[i]
+        return remote(ends[0], ends[1], self.send_sem.at[stage, c], self.recv_sem.at[stage, c], ends[2])
+
+    def first(self, c):
+        self.copy(0, c).start()
+
+    def second(self, c):
+        self.copy(0, c).wait_recv()
+        m, r1, core, mid = self.m, self.r1, self.core, self.mid
+        self.s2[c] = (m[c, core, 1 - mid].astype(F32) + r1[c, 1 - mid].astype(F32)).astype(BF16)
+        self.copy(1, c).start()
+        self.acc[c] = m[c, core, mid].astype(F32) + r1[c, mid].astype(F32)
+
+    def third(self, c):
+        self.copy(1, c).wait_recv()
+        self.acc[c] += self.r2[c].astype(F32)
+        own = self.s3.shape[2]
+        for a in range(self.nz):
+            for k in range(own):
+                block = self.acc[c, :, a * own + k, :]
+                self.s3f[c, a, k] = block
+                self.s3[c, a, k] = block.astype(BF16)
+        for i in range(1, self.nz):
+            self.copy(1 + i, c).start()
+
+    def advance(self, c):
+        self.first(c)
+        pl.when(c >= 1)(lambda: self.second(c - 1))
+        pl.when(c >= 2)(lambda: self.third(c - 2))
+
+    def close(self, own_ref):
+        parts, own = self.m.shape[0], self.s3.shape[2]
+        self.second(parts - 1)
+        self.third(parts - 2)
+        self.third(parts - 1)
+        for c in range(parts):
+            for i in range(1, self.nz):
+                self.copy(1 + i, c).wait_recv()
+            for k in range(own):
+                total = self.s3f[c, self.z, k]
+                for i in range(1, self.nz):
+                    total = total + self.r3[c, i, k].astype(F32)
+                own_ref[k, c * CHUNK : (c + 1) * CHUNK] = total
+
+    def finish(self):
+        for c in range(self.m.shape[0]):
+            for stage in range(self.nz + 1):
+                self.copy(stage, c).wait_send()
+
+
+class Small:
+    def __init__(self, scratch):
+        self.sm, self.rz, self.send_sem, self.recv_sem = scratch[18:22]
+        self.nz, _, _, _, self.z = place()
+        self.across, self.beside, _, self.line = peers()
+
+    def copy(self, stage):
+        if stage == 0:
+            ends = self.sm.at[0], self.sm.at[1], self.across
+        elif stage == 1:
+            ends = self.sm.at[2], self.sm.at[3], self.beside
+        else:
+            ends = self.rz.at[self.z], self.rz.at[self.z], self.line[stage - 1]
+        return remote(ends[0], ends[1], self.send_sem.at[stage], self.recv_sem.at[stage], ends[2])
+
+    def first(self):
+        self.copy(0).start()
+
+    def second(self):
+        self.copy(0).wait_recv()
+        self.sm[2] = self.sm[0] + self.sm[1]
+        self.copy(1).start()
+
+    def third(self):
+        self.copy(1).wait_recv()
+        self.rz[self.z] = self.sm[2] + self.sm[3]
+        for i in range(1, self.nz):
+            self.copy(1 + i).start()
+
+    def close(self, out_ref):
+        for i in range(1, self.nz):
+            self.copy(1 + i).wait_recv()
+        total = self.rz[0]
+        for i in range(1, self.nz):
+            total = total + self.rz[i]
+        out_ref[...] = total
+        for stage in range(self.nz + 1):
+            self.copy(stage).wait_send()
+
+
+def gather(scratch, mix, z_ref, small=None, small_ref=None):
+    zg, turn, zt = scratch[8:11]
+    send_sem, recv_sem = scratch[14:16]
+    nz, _, core, mid, z = place()
+    across, beside, _, line = peers()
+    own = zg.shape[2]
+    wide = zg.shape[0]
+
+    def link(stage, g, src, target):
+        return remote(src, src, send_sem.at[stage, g], recv_sem.at[stage, g], target)
+
+    copies = []
+    gathered = []
+    for g in range(wide):
+        mix(g, zg)
+        gathered.append([link(i, g, zg.at[g, z], line[i]) for i in range(1, nz)])
+        for copy in gathered[g]:
+            copy.start()
+    if small is not None:
+        small.close(small_ref)
+    sides = []
+    for g in range(wide):
+        for copy in gathered[g]:
             copy.wait_recv()
-        total = rz[0]
-        for i in range(1, nz):
-            total = total + rz[i]
-        small_ref[...] = total
-    for copy in gathered:
-        copy.wait_recv()
-    for a in range(nz):
-        for k in range(own):
-            acc[:, a * own + k, :] = zg[a, k].astype(F32)
-    zt[core, mid] = acc[...].astype(BF16)
-    side = links.start(zt.at[core, mid], zt.at[core, mid], beside)
-    near = links.start(zt.at[core, mid], zt.at[core, mid], across)
-    side.wait_recv()
-    far = links.start(zt.at[core, 1 - mid], zt.at[core, 1 - mid], across)
-    near.wait_recv()
-    far.wait_recv()
-    links.finish()
-    z_ref[...] = zt[...]
+        for a in range(nz):
+            for k in range(own):
+                turn[g, :, a * own + k, :] = zg[g, a, k].astype(F32)
+        zt[g, core, mid] = turn[g].astype(BF16)
+        side = link(0, g, zt.at[g, core, mid], beside)
+        near = link(nz, g, zt.at[g, core, mid], across)
+        side.start()
+        near.start()
+        sides.append((side, near))
+    fars = []
+    for g in range(wide):
+        sides[g][0].wait_recv()
+        far = link(nz + 1, g, zt.at[g, core, 1 - mid], across)
+        far.start()
+        fars.append(far)
+    for g in range(wide):
+        sides[g][1].wait_recv()
+        fars[g].wait_recv()
+        z_ref[:, :, g * HALF : (g + 1) * HALF] = zt[g]
+        for copy in gathered[g] + list(sides[g]) + [fars[g]]:
+            copy.wait_send()
 
 
 def mode_gain(me, own, k):
@@ -236,42 +320,43 @@
     return cat(b, a)
 
 
-def mix_forward(w_ref, me, x_ref, z_ref, z):
+def mix_forward(w_ref, me, x_ref, g, z_ref):
     own, chans = w_ref.shape[:2]
+    _, _, _, _, z = place()
     for k in range(own):
         x = x_ref[k]
         x_sw = swap(x)
-        first = jnp.zeros(w_ref.shape[2:], F32)
-        second = jnp.zeros(w_ref.shape[2:], F32)
+        first = jnp.zeros((HALF, LANES), F32)
+        second = jnp.zeros((HALF, LANES), F32)
         for c in range(chans):
-            w = w_ref[k, c]
+            w = w_ref[k, c, g * HALF : (g + 1) * HALF]
             first = first + x[c : c + 1] * w
             second = second + x_sw[c : c + 1] * w
         a, b = halves(first)
         c, d = halves(second)
-        z_ref[z, k] = (cat(a - b, c + d) * mode_gain(me, own, k)).astype(BF16)
-
-
-def mix_back(w_ref, me, d_ref, z_ref, z):
-    own, chans = w_ref.shape[:2]
+        z_ref[g, z, k] = (cat(a - b, c + d) * mode_gain(me, own, k)).astype(BF16)
+
+
+def mix_back(w_ref, me, d_ref, g, z_ref):
+    own = w_ref.shape[0]
+    _, _, _, _, z = place()
     for k in range(own):
-        d = d_ref[k] * mode_gain(me, own, k)
-        d_ref[k] = d
+        d = d_ref[k]
         d_sw = swap(d)
         firsts, seconds = [], []
-        for c in range(chans):
+        for c in range(g * HALF, (g + 1) * HALF):
             w = w_ref[k, c]
             firsts.append(jnp.sum(d * w, axis=0, keepdims=True))
             seconds.append(jnp.sum(d_sw * w, axis=0, keepdims=True))
         a, b = halves(jnp.concatenate(firsts, axis=0))
         e, f = halves(jnp.concatenate(seconds, axis=0))
-        z_ref[z, k] = cat(a + b, e - f).astype(BF16)
+        z_ref[g, z, k] = cat(a + b, e - f).astype(BF16)
 
 
 def analysis_kernel(x_ref, bt_ref, cols_ref, w_ref, z_ref, own_ref, cols, *scratch):
     step = pl.program_id(0)
     count, rows, width = x_ref.shape
-    m, wv, w_sem, c_sem = scratch[0], scratch[10], scratch[13], scratch[14]
+    m, wv, w_sem, c_sem = scratch[0], scratch[11], scratch[16], scratch[17]
     me = lax.axis_index("space")
     weights = pltpu.make_async_copy(w_ref, wv, w_sem)
     table = pltpu.make_async_copy(cols_ref.at[me], cols, c_sem)
@@ -287,13 +372,21 @@
     row_modes = dot(flat, bt_ref[...])
     modes = columns_of([row_modes[c * rows : (c + 1) * rows] for c in range(count)], cols[...]).astype(BF16)
     for c in range(count):
-        m[:, :, step * count + c] = modes[c * KY : (c + 1) * KY].reshape(2, 2, QUARTER, LANES)
+        m[step, :, :, c] = modes[c * KY : (c + 1) * KY].reshape(2, 2, QUARTER, LANES)
+
+    @pl.when(step == 0)
+    def _():
+        greeted()
+
+    sums = Sums(scratch)
+    sums.advance(step)
 
     @pl.when(step == pl.num_programs(0) - 1)
     def _():
-        greeted()
+        sums.close(own_ref)
         weights.wait()
-        exchange(scratch, functools.partial(mix_forward, wv, me), own_ref, z_ref)
+        gather(scratch, functools.partial(mix_forward, wv, me, own_ref), z_ref)
+        sums.finish()
 
 
 def whole(a):
@@ -310,7 +403,7 @@
 def analysis(x, bt, cols, weight, devices):
     chans, rows, width = x.shape
     own = weight.shape[0]
-    block = 8
+    block = CHUNK
     shapes = [
         jax.ShapeDtypeStruct((2, 2, chans, QUARTER, LANES), BF16),
         jax.ShapeDtypeStruct((own, chans, LANES), F32),
@@ -376,8 +469,7 @@
     slab = rows_ref.shape[1]
     half = chans * GROUP
     tile = 512
-    m, wv, w_sem, c_sem = scratch[0], scratch[10], scratch[13], scratch[14]
-    sm = scratch[15]
+    m, wv, w_sem, c_sem = scratch[0], scratch[11], scratch[16], scratch[17]
     me = lax.axis_index("space")
     weights = pltpu.make_async_copy(w_ref, wv, w_sem)
     table = pltpu.make_async_copy(cols_ref.at[me], cols, c_sem)
@@ -422,15 +514,6 @@
 
     @pl.when(step == pl.num_programs(0) - 1)
     def _():
-        count = 8
-
-        def body(i, carry):
-            modes = columns_of([rows_ref[i * count + k] for k in range(count)], cols[...]).astype(BF16)
-            for k in range(count):
-                m[:, :, i * count + k] = modes[k * KY : (k + 1) * KY].reshape(2, 2, QUARTER, LANES)
-            return carry
-
-        lax.fori_loop(0, chans // count, body, 0)
         first = lax.broadcasted_iota(jnp.int32, (half, half), 0) % GROUP
         second = lax.broadcasted_iota(jnp.int32, (half, half), 1) % GROUP
         kept = jnp.where(first == second, acc_ref[...], 0.0)
@@ -445,10 +528,28 @@
         terms = dot(hi, group) + (dot(lo, group) + dot(last, group))
         sums = jnp.sum(rows_ref[...], axis=1)[:, :1]
         lane = lax.broadcasted_iota(jnp.int32, (chans, LANES), 1)
-        sm[0] = jnp.where(lane == chans, sums, terms)
+        small = Small(scratch)
+        small.sm[0] = jnp.where(lane == chans, sums, terms)
         greeted()
+        small.first()
+        links = Sums(scratch)
+
+        def body(i, carry):
+            modes = columns_of([rows_ref[i * CHUNK + k] for k in range(CHUNK)], cols[...]).astype(BF16)
+            for k in range(CHUNK):
+                m[i, :, :, k] = modes[k * KY : (k + 1) * KY].reshape(2, 2, QUARTER, LANES)
+            links.advance(i)
+            return carry
+
+        lax.fori_loop(0, chans // CHUNK, body, 0)
+        small.second()
+        links.close(dm_ref)
+        small.third()
+        for k in range(dm_ref.shape[0]):
+            dm_ref[k] = dm_ref[k] * mode_gain(me, dm_ref.shape[0], k)
         weights.wait()
-        exchange(scratch, functools.partial(mix_back, wv, me), dm_ref, back_ref, small_ref)
+        gather(scratch, functools.partial(mix_back, wv, me, dm_ref), back_ref, small, small_ref)
+        links.finish()
 
 
 def forward(x, target, z, local_weight, bias, rb, bt, cols, weight, devices):

time: 114 us -> 111 us (0.974)
  Pallas kernels: 111 us -> 109 us
    pallas_call x1, Pallas kernels: 34.6 us -> 32.2 us  [analysis(): pl.pallas_call(analysis_kernel, grid=(chans // block,), in_specs=[pl.Bloc...]
where the time goes in v4:
time: 111 us
  Pallas kernels  109 us (98%)
  local copies, waits for them, and re-layouts  1.33 us (1%)
    pallas_call x1, Pallas kernels, forward(): pl.pallas_call(forward_kernel, grid=(slab // ROWS,), in_specs=[band, band...  55.9 us
    pallas_call x1, Pallas kernels, analysis(): pl.pallas_call(analysis_kernel, grid=(chans // block,), in_specs=[pl.Bloc...  32.2 us
    pallas_call x1, Pallas kernels, final(): pl.pallas_call(functools.partial(final_kernel, math.sqrt(cells_count), ce...  20.8 us

profile of v4, /device:TPU:0, one launch (start us, length us, event | category | flops | bytes accessed | tf_op | source)
XLA Modules:
  0.0 110.9 jit_solution(6793161722723162145)
XLA Ops:
  0.6 1.3 %broadcast_in_dim.2.bias_ref = f32[32,128]{1,0:T(8,128)} broadcast(f32[32]{0:T(128)} %param.13), dimensions={0} | broadcast | bytes 16512 | tf_op jit(solution)/shard_map/broadcast_in_dim | solution.py:675
  2.0 32.2 %analysis.1 = (bf16[2,2,32,16,128]{4,3,2,1,0:T(8,128)(2,1)}, f32[4,32,128]{2,1,0:T(8,128)}) custom-call(bf16[32,128,2048]{2,1,0:T(8,128)(2,1)} %bitcast.6, bf16[2048,128]{1,0:T(8,128)(2,1)} %constant.9.clone.bt_ref, bf16[16,256,256]{2,1,0:T(8,128)(2,1)} %constant.11.clone.cols_ref, f32[4,32,32,128]{3,2,1,0:T(8,128)} %w_ref.3), custom_call_target="tpu_custom_call" | custom-call | tf_op jit(solution)/shard_map/analysis/pallas_call | solution.py:411
  34.2 55.9 %forward.1 = (bf16[32,128,2048]{2,1,0:T(8,128)(2,1)}, bf16[2,2,32,16,128]{4,3,2,1,0:T(8,128)(2,1)}, f32[4,32,128]{2,1,0:T(8,128)}, f32[32,128]{1,0:T(8,128)}) custom-call(bf16[32,128,2048]{2,1,0:T(8,128)(2,1)} %bitcast.7, bf16[32,128,2048]{2,1,0:T(8,128)(2,1)} %bitcast.8, bf16[2,2,32,16,128]{4,3,2,1,0:T(8,128)(2,1)} %get-tuple-element.14.z_ref, ...), custom_call_target="tpu_custom_call" | custom-call | tf_op jit(solution)/shard_map/forward/pallas_call | solution.py:566
  90.1 20.8 %final.1 = (bf16[32,128,2048]{2,1,0:T(8,128)(2,1)}, f32[128,32,128]{2,1,0:T(8,128)}, f32[32,32]{1,0:T(8,128)}, f32[1,32]{1,0:T(1,128)}) custom-call(bf16[32,128,2048]{2,1,0:T(8,128)(2,1)} %get-tuple-element.15.d_ref, bf16[2,2,32,16,128]{4,3,2,1,0:T(8,128)(2,1)} %get-tuple-element.16.z_ref, bf16[32,32]{1,0:T(8,128)(2,1)} %lw_ref.3, ...), custom_call_target="tpu_custom_call" | custom-call | tf_op jit(solution)/shard_map/final/pallas_call | solution.py:636

commit v5 on v4

--- a/solution.py
+++ b/solution.py
@@ -20,6 +20,9 @@
 GROUP = 8
 CHUNK = 8
 HALF = 16
+THIRD = 1
+MIX = 4
+LAST_ROWS = 32
 F32 = jnp.float32
 BF16 = jnp.bfloat16
 NT = (((1,), (1,)), ((), ()))
@@ -206,9 +209,6 @@
 
     def close(self, own_ref):
         parts, own = self.m.shape[0], self.s3.shape[2]
-        self.second(parts - 1)
-        self.third(parts - 2)
-        self.third(parts - 1)
         for c in range(parts):
             for i in range(1, self.nz):
                 self.copy(1 + i, c).wait_recv()
@@ -264,51 +264,52 @@
             self.copy(stage).wait_send()
 
 
-def gather(scratch, mix, z_ref, small=None, small_ref=None):
-    zg, turn, zt = scratch[8:11]
-    send_sem, recv_sem = scratch[14:16]
-    nz, _, core, mid, z = place()
-    across, beside, _, line = peers()
-    own = zg.shape[2]
-    wide = zg.shape[0]
-
-    def link(stage, g, src, target):
-        return remote(src, src, send_sem.at[stage, g], recv_sem.at[stage, g], target)
-
-    copies = []
-    gathered = []
-    for g in range(wide):
-        mix(g, zg)
-        gathered.append([link(i, g, zg.at[g, z], line[i]) for i in range(1, nz)])
-        for copy in gathered[g]:
-            copy.start()
-    if small is not None:
-        small.close(small_ref)
-    sides = []
-    for g in range(wide):
-        for copy in gathered[g]:
-            copy.wait_recv()
-        for a in range(nz):
-            for k in range(own):
-                turn[g, :, a * own + k, :] = zg[g, a, k].astype(F32)
-        zt[g, core, mid] = turn[g].astype(BF16)
-        side = link(0, g, zt.at[g, core, mid], beside)
-        near = link(nz, g, zt.at[g, core, mid], across)
-        side.start()
-        near.start()
-        sides.append((side, near))
-    fars = []
-    for g in range(wide):
-        sides[g][0].wait_recv()
-        far = link(nz + 1, g, zt.at[g, core, 1 - mid], across)
-        far.start()
-        fars.append(far)
-    for g in range(wide):
-        sides[g][1].wait_recv()
-        fars[g].wait_recv()
-        z_ref[:, :, g * HALF : (g + 1) * HALF] = zt[g]
-        for copy in gathered[g] + list(sides[g]) + [fars[g]]:
-            copy.wait_send()
+class Gather:
+    def __init__(self, scratch):
+        self.zg, self.turn, self.zt = scratch[8:11]
+        self.send_sem, self.recv_sem = scratch[14:16]
+        self.nz, _, self.core, self.mid, self.z = place()
+        self.across, self.beside, _, self.line = peers()
+        self.wide = self.zg.shape[0]
+
+    def copy(self, stage, g):
+        if stage == 0:
+            src, target = self.zt.at[g, self.core, self.mid], self.beside
+        elif stage < self.nz:
+            src, target = self.zg.at[g, self.z], self.line[stage]
+        elif stage == self.nz:
+            src, target = self.zt.at[g, self.core, self.mid], self.across
+        else:
+            src, target = self.zt.at[g, self.core, 1 - self.mid], self.across
+        return remote(src, src, self.send_sem.at[stage, g], self.recv_sem.at[stage, g], target)
+
+    def first(self, mix):
+        for g in range(self.wide):
+            mix(g, self.zg)
+            for i in range(1, self.nz):
+                self.copy(i, g).start()
+
+    def close(self, z_ref):
+        zg, turn, zt = self.zg, self.turn, self.zt
+        own = zg.shape[2]
+        for g in range(self.wide):
+            for i in range(1, self.nz):
+                self.copy(i, g).wait_recv()
+            for a in range(self.nz):
+                for k in range(own):
+                    turn[g, :, a * own + k, :] = zg[g, a, k].astype(F32)
+            zt[g, self.core, self.mid] = turn[g].astype(BF16)
+            self.copy(0, g).start()
+            self.copy(self.nz, g).start()
+        for g in range(self.wide):
+            self.copy(0, g).wait_recv()
+            self.copy(self.nz + 1, g).start()
+        for g in range(self.wide):
+            self.copy(self.nz, g).wait_recv()
+            self.copy(self.nz + 1, g).wait_recv()
+            z_ref[:, :, g * HALF : (g + 1) * HALF] = zt[g]
+            for stage in range(self.nz + 2):
+                self.copy(stage, g).wait_send()
 
 
 def mode_gain(me, own, k):
@@ -383,9 +384,14 @@
 
     @pl.when(step == pl.num_programs(0) - 1)
     def _():
+        sums.second(step)
+        sums.third(step - 1)
+        sums.third(step)
         sums.close(own_ref)
         weights.wait()
-        gather(scratch, functools.partial(mix_forward, wv, me, own_ref), z_ref)
+        gather = Gather(scratch)
+        gather.first(functools.partial(mix_forward, wv, me, own_ref))
+        gather.close(z_ref)
         sums.finish()
 
 
@@ -463,8 +469,10 @@
 
 
 def forward_kernel(x_ref, t_ref, z_ref, lw_ref, bias_ref, rb_ref, bt_ref, cols_ref, w_ref,
-                   delta_ref, back_ref, dm_ref, small_ref, cols, kron, rows_ref, acc_ref, e_ref, *scratch):
+                   part_ref, back_ref, dm_ref, small_ref, cols, kron, kron_back, delta_ref, rows_ref, acc_ref, e_ref,
+                   *scratch):
     step = pl.program_id(0)
+    bands = pl.num_programs(0) // 2
     chans, rows, width = x_ref.shape
     slab = rows_ref.shape[1]
     half = chans * GROUP
@@ -481,38 +489,49 @@
         weights.start()
         acc_ref[...] = jnp.zeros_like(acc_ref)
         kron[...] = spread(lw_ref[...], True, 0.5)
+        kron_back[...] = spread(lw_ref[...], False, 0.5)
         table.wait()
         expand_rows(z_ref, cols[...], slab, e_ref)
 
-    bias = jnp.broadcast_to((bias_ref[...] * 0.5)[:, None, :], (chans, GROUP, LANES)).reshape(half, LANES)
-    bias = bias_block(bias)
-    def one_band(i, carry):
-        first = pl.multiple_of(i * BAND, BAND)
-        here = pl.ds(first, BAND)
-        band = pl.ds(pl.multiple_of(step * rows + first, BAND), BAND)
+    @pl.when(step < bands)
+    def _():
+        bias = jnp.broadcast_to((bias_ref[...] * 0.5)[:, None, :], (chans, GROUP, LANES)).reshape(half, LANES)
+        bias = bias_block(bias)
+        band = pl.ds(pl.multiple_of(step * rows, rows), rows)
         e = (e_ref[:, band, :].astype(F32) * 0.5).astype(BF16)
         left = [cat(group, bias) for group in groups_of(e)]
         deltas = []
         for start in range(0, width, tile):
             cells = pl.ds(start, tile)
             sums = []
-            for lhs, x in zip(left, groups_of(x_ref[:, here, cells])):
+            for lhs, x in zip(left, groups_of(x_ref[:, :, cells])):
                 sums.append(dot(kron[...], x) + dot(lhs, rb_ref[:, cells]))
-            delta = twice_delta(joined(sums, chans).astype(BF16), t_ref[:, here, cells])
-            delta_ref[:, here, cells] = delta
+            delta = twice_delta(joined(sums, chans).astype(BF16), t_ref[:, :, cells])
+            delta_ref[:, band, cells] = delta
             deltas.append(groups_of(delta))
         row_modes = []
-        for g, x in enumerate(groups_of(x_ref[:, here, :])):
+        for g, x in enumerate(groups_of(x_ref[...])):
             delta = jnp.concatenate([d[g] for d in deltas], axis=1)
             both = dot_nt(jnp.concatenate([x, bt_ref[...]], axis=0), delta)
             acc_ref[...] += both[:half]
             row_modes.append(both[half:].T)
         rows_ref[:, band, :] = joined(row_modes, chans) * 0.5
-        return carry
-
-    lax.fori_loop(0, rows // BAND, one_band, 0)
-
-    @pl.when(step == pl.num_programs(0) - 1)
+
+    @pl.when(step >= bands)
+    def _():
+        band = pl.ds(pl.multiple_of((step - bands) * rows, rows), rows)
+        for start in range(0, width, tile):
+            cells = pl.ds(start, tile)
+            out = [dot(kron_back[...], d) for d in groups_of(delta_ref[:, band, cells])]
+            part_ref[:, :, cells] = joined(out, chans).astype(BF16)
+
+    small = Small(scratch)
+    links = Sums(scratch)
+    gather = Gather(scratch)
+    own = dm_ref.shape[0]
+    chunks = chans // CHUNK
+
+    @pl.when(step == bands - 1)
     def _():
         first = lax.broadcasted_iota(jnp.int32, (half, half), 0) % GROUP
         second = lax.broadcasted_iota(jnp.int32, (half, half), 1) % GROUP
@@ -528,27 +547,40 @@
         terms = dot(hi, group) + (dot(lo, group) + dot(last, group))
         sums = jnp.sum(rows_ref[...], axis=1)[:, :1]
         lane = lax.broadcasted_iota(jnp.int32, (chans, LANES), 1)
-        small = Small(scratch)
         small.sm[0] = jnp.where(lane == chans, sums, terms)
         greeted()
         small.first()
-        links = Sums(scratch)
 
         def body(i, carry):
             modes = columns_of([rows_ref[i * CHUNK + k] for k in range(CHUNK)], cols[...]).astype(BF16)
             for k in range(CHUNK):
                 m[i, :, :, k] = modes[k * KY : (k + 1) * KY].reshape(2, 2, QUARTER, LANES)
-            links.advance(i)
+            links.first(i)
+            pl.when(i >= 1)(lambda: links.second(i - 1))
             return carry
 
-        lax.fori_loop(0, chans // CHUNK, body, 0)
+        lax.fori_loop(0, chunks, body, 0)
+        links.second(chunks - 1)
         small.second()
+
+    @pl.when(step == bands + jnp.minimum(THIRD, bands - 1))
+    def _():
+        for c in range(chunks):
+            links.third(c)
+        small.third()
+
+    @pl.when(step == bands + jnp.minimum(MIX, bands - 1))
+    def _():
         links.close(dm_ref)
-        small.third()
-        for k in range(dm_ref.shape[0]):
-            dm_ref[k] = dm_ref[k] * mode_gain(me, dm_ref.shape[0], k)
+        for k in range(own):
+            dm_ref[k] = dm_ref[k] * mode_gain(me, own, k)
         weights.wait()
-        gather(scratch, functools.partial(mix_back, wv, me, dm_ref), back_ref, small, small_ref)
+        gather.first(functools.partial(mix_back, wv, me, dm_ref))
+
+    @pl.when(step == pl.num_programs(0) - 1)
+    def _():
+        gather.close(back_ref)
+        small.close(small_ref)
         links.finish()
 
 
@@ -556,7 +588,9 @@
     chans, slab, width = x.shape
     own = weight.shape[0]
     half = chans * GROUP
-    band = pl.BlockSpec((chans, ROWS, width), lambda i: (0, i, 0))
+    bands = slab // ROWS
+    band = pl.BlockSpec((chans, ROWS, width), lambda i: (0, jnp.minimum(i, bands - 1), 0))
+    later = pl.BlockSpec((chans, ROWS, width), lambda i: (0, jnp.maximum(i - bands, 0), 0))
     shapes = [
         jax.ShapeDtypeStruct(x.shape, BF16),
         jax.ShapeDtypeStruct((2, 2, chans, QUARTER, LANES), BF16),
@@ -565,13 +599,15 @@
     ]
     return pl.pallas_call(
         forward_kernel,
-        grid=(slab // ROWS,),
+        grid=(2 * bands,),
         in_specs=[band, band, whole(z), whole(local_weight), whole(bias), whole(rb), whole(bt), HBM, HBM],
-        out_specs=[band] + [held(s.shape) for s in shapes[1:]],
+        out_specs=[later] + [held(s.shape) for s in shapes[1:]],
         out_shape=shapes,
         scratch_shapes=[
             pltpu.VMEM(cols.shape[1:], BF16),
             pltpu.VMEM((half, half), BF16),
+            pltpu.VMEM((half, half), BF16),
+            pltpu.VMEM((chans, slab, width), BF16),
             pltpu.VMEM((chans, slab, 2 * KY), F32),
             pltpu.VMEM((half, half), F32),
             pltpu.VMEM((chans, slab, 2 * KY), BF16),
@@ -581,10 +617,10 @@
     )(x, target, z, local_weight, bias, rb, bt, cols, weight)
 
 
-def final_kernel(root, cells_count, d_ref, z_ref, lw_ref, rb_ref, cols_ref, xm_ref, dm_ref, small_ref,
-                 out_ref, g_ref, local_ref, bias_ref, cols, kron, e_ref, c_sem):
+def final_kernel(root, cells_count, part_ref, z_ref, rb_ref, cols_ref, xm_ref, dm_ref, small_ref,
+                 out_ref, g_ref, local_ref, bias_ref, cols, e_ref, c_sem):
     step = pl.program_id(0)
-    chans, rows, width = d_ref.shape
+    chans, rows, width = part_ref.shape
     slab = e_ref.shape[1]
     tile = 512
     pairs = g_ref.shape[0]
@@ -594,7 +630,6 @@
     @pl.when(step == 0)
     def _():
         table.start()
-        kron[...] = spread(lw_ref[...], False, 0.5)
         small = small_ref[...]
         local_ref[...] = small[:, :chans] * (1.0 / cells_count)
         column = small[:, chans : chans + 1] * (root / cells_count)
@@ -607,13 +642,12 @@
         first = pl.multiple_of(i * BAND, BAND)
         here = pl.ds(first, BAND)
         e = e_ref[:, pl.ds(pl.multiple_of(step * rows + first, BAND), BAND), :]
-        left = [cat(kron[...], group) for group in groups_of(e)]
+        e = e.reshape(chans * BAND, LANES)
         for start in range(0, width, tile):
             cells = pl.ds(start, tile)
-            out = []
-            for lhs, d in zip(left, groups_of(d_ref[:, here, cells])):
-                out.append(dot(lhs, jnp.concatenate([d, rb_ref[:, cells]], axis=0)))
-            out_ref[:, here, cells] = joined(out, chans).astype(BF16)
+            part = part_ref[:, here, cells].reshape(chans * BAND, tile).astype(F32)
+            out = dot(e, rb_ref[:, cells]) + part
+            out_ref[:, here, cells] = out.astype(BF16).reshape(chans, BAND, tile)
         return carry
 
     lax.fori_loop(0, rows // BAND, one_band, 0)
@@ -625,18 +659,18 @@
         g_ref[i] = cat(re, re) * d + cat(im, -im) * swap(d)
 
 
-def final(delta, z, local_weight, rb, cols, own_modes, delta_modes, small, height):
-    chans, slab, width = delta.shape
+def final(part, z, rb, cols, own_modes, delta_modes, small, height):
+    chans, slab, width = part.shape
     own = own_modes.shape[0]
-    steps = slab // ROWS
+    steps = slab // LAST_ROWS
     pairs = own * chans // steps
-    band = pl.BlockSpec((chans, ROWS, width), lambda i: (0, i, 0))
+    band = pl.BlockSpec((chans, LAST_ROWS, width), lambda i: (0, i, 0))
     own_modes = own_modes.reshape(own * chans, LANES)
     cells_count = height * width
     return pl.pallas_call(
         functools.partial(final_kernel, math.sqrt(cells_count), cells_count),
         grid=(steps,),
-        in_specs=[band, whole(z), whole(local_weight), whole(rb), HBM, whole(own_modes), whole(delta_modes), whole(small)],
+        in_specs=[band, whole(z), whole(rb), HBM, whole(own_modes), whole(delta_modes), whole(small)],
         out_specs=[
             band,
             pl.BlockSpec((pairs, chans, LANES), lambda i: (i, 0, 0)),
@@ -644,20 +678,19 @@
             held((1, chans)),
         ],
         out_shape=[
-            jax.ShapeDtypeStruct(delta.shape, BF16),
+            jax.ShapeDtypeStruct(part.shape, BF16),
             jax.ShapeDtypeStruct((own * chans, chans, LANES), F32),
             jax.ShapeDtypeStruct((chans, chans), F32),
             jax.ShapeDtypeStruct((1, chans), F32),
         ],
         scratch_shapes=[
             pltpu.VMEM(cols.shape[1:], BF16),
-            pltpu.VMEM((chans * GROUP, chans * GROUP), BF16),
             pltpu.VMEM((chans, slab, 2 * KY), BF16),
             pltpu.SemaphoreType.DMA,
         ],
         compiler_params=pltpu.CompilerParams(vmem_limit_bytes=LIMIT),
         name="final",
-    )(delta, z, local_weight, rb, cols, own_modes, delta_modes, small)
+    )(part, z, rb, cols, own_modes, delta_modes, small)
 
 
 def per_device(inputs, target, spectral_weight, local_weight, bias_term):
@@ -676,11 +709,11 @@
 
     x = inputs.reshape(chans, slab, width)
     z, own_modes = analysis(x, bt, cols, spectral_weight, devices)
-    delta, z, delta_modes, small = forward(
+    part, z, delta_modes, small = forward(
         x, target.reshape(chans, slab, width), z, local_weight, bias, rb_bias, rb, cols, spectral_weight, devices
     )
     grad_input, grad_spectral, grad_local, grad_bias = final(
-        delta, z, local_weight, rb, cols, own_modes, delta_modes, small, height
+        part, z, rb, cols, own_modes, delta_modes, small, height
     )
     return (
         grad_input.reshape(inputs.shape),

time: 111 us -> 106 us (0.955)
  Pallas kernels: 109 us -> 104 us
    pallas_call x1, Pallas kernels: 20.8 us -> 17.7 us  [final(): pl.pallas_call(functools.partial(final_kernel, math.sqrt(cells_count), ce...]
    pallas_call x1, Pallas kernels: 55.9 us -> 54 us  [forward(): pl.pallas_call(forward_kernel, grid=(2 * bands,), in_specs=[band, band, w...]
where the time goes in v5:
time: 106 us
  Pallas kernels  104 us (98%)
  local copies, waits for them, and re-layouts  1.33 us (1%)
    pallas_call x1, Pallas kernels, forward(): pl.pallas_call(forward_kernel, grid=(2 * bands,), in_specs=[band, band, w...  54 us
    pallas_call x1, Pallas kernels, analysis(): pl.pallas_call(analysis_kernel, grid=(chans // block,), in_specs=[pl.Bloc...  32.2 us
    pallas_call x1, Pallas kernels, final(): pl.pallas_call(functools.partial(final_kernel, math.sqrt(cells_count), ce...  17.7 us

profile of v5, /device:TPU:0, one launch (start us, length us, event | category | flops | bytes accessed | tf_op | source)
XLA Modules:
  0.0 105.9 jit_solution(13469425795439668654)
XLA Ops:
  0.6 1.3 %broadcast_in_dim.2.bias_ref = f32[32,128]{1,0:T(8,128)} broadcast(f32[32]{0:T(128)} %param.13), dimensions={0} | broadcast | bytes 16512 | tf_op jit(solution)/shard_map/broadcast_in_dim | solution.py:708
  2.0 32.2 %analysis.1 = (bf16[2,2,32,16,128]{4,3,2,1,0:T(8,128)(2,1)}, f32[4,32,128]{2,1,0:T(8,128)}) custom-call(bf16[32,128,2048]{2,1,0:T(8,128)(2,1)} %bitcast.6, bf16[2048,128]{1,0:T(8,128)(2,1)} %constant.9.clone.bt_ref, bf16[16,256,256]{2,1,0:T(8,128)(2,1)} %constant.11.clone.cols_ref, f32[4,32,32,128]{3,2,1,0:T(8,128)} %w_ref.3), custom_call_target="tpu_custom_call" | custom-call | tf_op jit(solution)/shard_map/analysis/pallas_call | solution.py:417
  34.2 54.0 %forward.1 = (bf16[32,128,2048]{2,1,0:T(8,128)(2,1)}, bf16[2,2,32,16,128]{4,3,2,1,0:T(8,128)(2,1)}, f32[4,32,128]{2,1,0:T(8,128)}, f32[32,128]{1,0:T(8,128)}) custom-call(bf16[32,128,2048]{2,1,0:T(8,128)(2,1)} %bitcast.7, bf16[32,128,2048]{2,1,0:T(8,128)(2,1)} %bitcast.8, bf16[2,2,32,16,128]{4,3,2,1,0:T(8,128)(2,1)} %get-tuple-element.14.z_ref, ...), custom_call_target="tpu_custom_call" | custom-call | tf_op jit(solution)/shard_map/forward/pallas_call | solution.py:600
  88.2 17.7 %final.1 = (bf16[32,128,2048]{2,1,0:T(8,128)(2,1)}, f32[128,32,128]{2,1,0:T(8,128)}, f32[32,32]{1,0:T(8,128)}, f32[1,32]{1,0:T(1,128)}) custom-call(bf16[32,128,2048]{2,1,0:T(8,128)(2,1)} %get-tuple-element.15.part_ref, bf16[2,2,32,16,128]{4,3,2,1,0:T(8,128)(2,1)} %get-tuple-element.16.z_ref, bf16[128,2048]{1,0:T(8,128)(2,1)} %constant.8.clone.bt_ref.rb_ref, ...), custom_call_target="tpu_custom_call" | custom-call | tf_op jit(solution)/shard_map/final/pallas_call | solution.py:670

commit v6 on v5

--- a/solution.py
+++ b/solution.py
@@ -469,7 +469,7 @@
 
 
 def forward_kernel(x_ref, t_ref, z_ref, lw_ref, bias_ref, rb_ref, bt_ref, cols_ref, w_ref,
-                   part_ref, back_ref, dm_ref, small_ref, cols, kron, kron_back, delta_ref, rows_ref, acc_ref, e_ref,
+                   part_ref, back_ref, dm_ref, small_ref, cols, kron, kron_back, bias_wide, delta_ref, rows_ref, acc_ref, e_ref,
                    *scratch):
     step = pl.program_id(0)
     bands = pl.num_programs(0) // 2
@@ -490,16 +490,18 @@
         acc_ref[...] = jnp.zeros_like(acc_ref)
         kron[...] = spread(lw_ref[...], True, 0.5)
         kron_back[...] = spread(lw_ref[...], False, 0.5)
+        eye = lax.broadcasted_iota(jnp.int32, (half, chans), 0) // GROUP
+        eye = eye == lax.broadcasted_iota(jnp.int32, (half, chans), 1)
+        column = jnp.sum(jnp.where(eye, bias_ref[...] * 0.5, 0.0), axis=1, keepdims=True)
+        bias_wide[...] = bias_block(jnp.broadcast_to(column, (half, LANES)))
         table.wait()
         expand_rows(z_ref, cols[...], slab, e_ref)
 
     @pl.when(step < bands)
     def _():
-        bias = jnp.broadcast_to((bias_ref[...] * 0.5)[:, None, :], (chans, GROUP, LANES)).reshape(half, LANES)
-        bias = bias_block(bias)
         band = pl.ds(pl.multiple_of(step * rows, rows), rows)
         e = (e_ref[:, band, :].astype(F32) * 0.5).astype(BF16)
-        left = [cat(group, bias) for group in groups_of(e)]
+        left = [cat(group, bias_wide[...]) for group in groups_of(e)]
         deltas = []
         for start in range(0, width, tile):
             cells = pl.ds(start, tile)
@@ -607,6 +609,7 @@
             pltpu.VMEM(cols.shape[1:], BF16),
             pltpu.VMEM((half, half), BF16),
             pltpu.VMEM((half, half), BF16),
+            pltpu.VMEM((half, LANES), BF16),
             pltpu.VMEM((chans, slab, width), BF16),
             pltpu.VMEM((chans, slab, 2 * KY), F32),
             pltpu.VMEM((half, half), F32),
@@ -705,7 +708,7 @@
     ones[:3] = 1.0
     rb_bias = jnp.asarray(np.concatenate([table, ones]))
     cols = jnp.asarray(column_table(height, devices))
-    bias = jnp.broadcast_to(bias_term[:, None], (chans, LANES))
+    bias = bias_term.reshape(1, chans)
 
     x = inputs.reshape(chans, slab, width)
     z, own_modes = analysis(x, bt, cols, spectral_weight, devices)

time: 106 us -> 105 us (level)
  local copies, waits for them, and re-layouts: 1.33 us -> 0 us
    broadcast_in_dim x1 -> x0, local copies, waits for them, and re-layouts: 1.33 us -> none  [per_device(): bias = jnp.broadcast_to(bias_term[:, None], (chans, LANES))]
where the time goes in v6:
time: 105 us
  Pallas kernels  104 us (99%)
    pallas_call x1, Pallas kernels, forward(): pl.pallas_call(forward_kernel, grid=(2 * bands,), in_specs=[band, band, w...  54 us
    pallas_call x1, Pallas kernels, analysis(): pl.pallas_call(analysis_kernel, grid=(chans // block,), in_specs=[pl.Bloc...  32.3 us
    pallas_call x1, Pallas kernels, final(): pl.pallas_call(functools.partial(final_kernel, math.sqrt(cells_count), ce...  17.7 us

profile of v6, /device:TPU:0, one launch (start us, length us, event | category | flops | bytes accessed | tf_op | source)
XLA Modules:
  0.0 104.7 jit_solution(11566157408318547596)
XLA Ops:
  0.6 32.3 %analysis.1 = (bf16[2,2,32,16,128]{4,3,2,1,0:T(8,128)(2,1)}, f32[4,32,128]{2,1,0:T(8,128)}) custom-call(bf16[32,128,2048]{2,1,0:T(8,128)(2,1)} %bitcast.7, bf16[2048,128]{1,0:T(8,128)(2,1)} %constant.9.clone.bt_ref, bf16[16,256,256]{2,1,0:T(8,128)(2,1)} %constant.11.clone.cols_ref, f32[4,32,32,128]{3,2,1,0:T(8,128)} %w_ref.3), custom_call_target="tpu_custom_call" | custom-call | tf_op jit(solution)/shard_map/analysis/pallas_call | solution.py:417
  32.9 54.0 %forward.1 = (bf16[32,128,2048]{2,1,0:T(8,128)(2,1)}, bf16[2,2,32,16,128]{4,3,2,1,0:T(8,128)(2,1)}, f32[4,32,128]{2,1,0:T(8,128)}, f32[32,128]{1,0:T(8,128)}) custom-call(bf16[32,128,2048]{2,1,0:T(8,128)(2,1)} %bitcast.8, bf16[32,128,2048]{2,1,0:T(8,128)(2,1)} %bitcast.9, bf16[2,2,32,16,128]{4,3,2,1,0:T(8,128)(2,1)} %get-tuple-element.14.z_ref, ...), custom_call_target="tpu_custom_call" | custom-call | tf_op jit(solution)/shard_map/forward/pallas_call | solution.py:602
  86.9 17.7 %final.1 = (bf16[32,128,2048]{2,1,0:T(8,128)(2,1)}, f32[128,32,128]{2,1,0:T(8,128)}, f32[32,32]{1,0:T(8,128)}, f32[1,32]{1,0:T(1,128)}) custom-call(bf16[32,128,2048]{2,1,0:T(8,128)(2,1)} %get-tuple-element.15.part_ref, bf16[2,2,32,16,128]{4,3,2,1,0:T(8,128)(2,1)} %get-tuple-element.16.z_ref, bf16[128,2048]{1,0:T(8,128)(2,1)} %constant.8.clone.bt_ref.rb_ref, ...), custom_call_target="tpu_custom_call" | custom-call | tf_op jit(solution)/shard_map/final/pallas_call | solution.py:673

commit v7 on v6

--- a/solution.py
+++ b/solution.py
@@ -77,7 +77,7 @@
 def expand_rows(z_ref, table, slab, e_ref):
     chans = z_ref.shape[2]
     left = table[:slab]
-    pair = 8
+    pair = 32
 
     def body(i, carry):
         parts = []

time: 105 us -> 104 us (level)
  no operation moved by 1% of the time
where the time goes in v7:
time: 104 us
  Pallas kernels  103 us (99%)
    pallas_call x1, Pallas kernels, forward(): pl.pallas_call(forward_kernel, grid=(2 * bands,), in_specs=[band, band, w...  53.5 us
    pallas_call x1, Pallas kernels, analysis(): pl.pallas_call(analysis_kernel, grid=(chans // block,), in_specs=[pl.Bloc...  32.3 us
    pallas_call x1, Pallas kernels, final(): pl.pallas_call(functools.partial(final_kernel, math.sqrt(cells_count), ce...  17.1 us

profile of v7, /device:TPU:0, one launch (start us, length us, event | category | flops | bytes accessed | tf_op | source)
XLA Modules:
  0.0 103.5 jit_solution(9020565208479448985)
XLA Ops:
  0.6 32.3 %analysis.1 = (bf16[2,2,32,16,128]{4,3,2,1,0:T(8,128)(2,1)}, f32[4,32,128]{2,1,0:T(8,128)}) custom-call(bf16[32,128,2048]{2,1,0:T(8,128)(2,1)} %bitcast.7, bf16[2048,128]{1,0:T(8,128)(2,1)} %constant.9.clone.bt_ref, bf16[16,256,256]{2,1,0:T(8,128)(2,1)} %constant.11.clone.cols_ref, f32[4,32,32,128]{3,2,1,0:T(8,128)} %w_ref.3), custom_call_target="tpu_custom_call" | custom-call | tf_op jit(solution)/shard_map/analysis/pallas_call | solution.py:417
  32.9 53.5 %forward.1 = (bf16[32,128,2048]{2,1,0:T(8,128)(2,1)}, bf16[2,2,32,16,128]{4,3,2,1,0:T(8,128)(2,1)}, f32[4,32,128]{2,1,0:T(8,128)}, f32[32,128]{1,0:T(8,128)}) custom-call(bf16[32,128,2048]{2,1,0:T(8,128)(2,1)} %bitcast.8, bf16[32,128,2048]{2,1,0:T(8,128)(2,1)} %bitcast.9, bf16[2,2,32,16,128]{4,3,2,1,0:T(8,128)(2,1)} %get-tuple-element.14.z_ref, ...), custom_call_target="tpu_custom_call" | custom-call | tf_op jit(solution)/shard_map/forward/pallas_call | solution.py:602
  86.4 17.1 %final.1 = (bf16[32,128,2048]{2,1,0:T(8,128)(2,1)}, f32[128,32,128]{2,1,0:T(8,128)}, f32[32,32]{1,0:T(8,128)}, f32[1,32]{1,0:T(1,128)}) custom-call(bf16[32,128,2048]{2,1,0:T(8,128)(2,1)} %get-tuple-element.15.part_ref, bf16[2,2,32,16,128]{4,3,2,1,0:T(8,128)(2,1)} %get-tuple-element.16.z_ref, bf16[128,2048]{1,0:T(8,128)(2,1)} %constant.8.clone.bt_ref.rb_ref, ...), custom_call_target="tpu_custom_call" | custom-call | tf_op jit(solution)/shard_map/final/pallas_call | solution.py:673
